TPU v7x, 128 devices: a whole 4x4x4 slice. The times are simulated.
128 devices in a mesh: src: 16 (over x, y), unit: 8 (over z, core).
Axes of the slice: x: 4, y: 4, z: 4, core: 2. Of those that a mesh axis runs over, the one named last changes fastest.
Arguments:
- coeffs: float32 [384, 55], P('src'), may hold values from -6 to 6
- spectra: bfloat16 [131072, 60], P(('src', 'unit')), may hold values from -6 to 6
- epoch_weight: bfloat16 [131072], P(('src', 'unit')), may hold values from 0.25 to 4
- source_blocks: int32 [16, 24], P('src'), may hold values from 1 to 8, 64 in all within a row
- epoch_owner: int32 [131072, 1], P(('src', 'unit')), may hold values from 0 to 7; in each aligned block of 1024 rows (0 to 1023, 1024 to 2047, ...) at most 256 rows name the same one
- epoch_unit_local: int32 [131072], P(('src', 'unit')), may hold values from 0 to 255
- design: bfloat16 [2048, 3300], P('unit'), may hold values from -0.875 to 0.875
Outputs:
- new_design: float32 [2048, 3300], P('unit')
- new_coeffs: float32 [384, 55], P('src')
Inputs may be any that keep to these rules, and one draw needn't show every extreme that they name: Each row of source_blocks sums to 64 and holds the value 8. `epoch_owner`: in the rows of one device no value appears more than 256 times, and one value appears exactly 256 times.
All inputs are finite; a program needn't handle non-finite values.
Results may differ from a plain program's by a relative error of at most 0.0045.
Values may be sent and summed in bfloat16 or wider, within the bound.
A program may use at most 64 MiB of HBM per device.

v0:
```python
import jax
import jax.numpy as jnp
from jax import lax
from jax.sharding import PartitionSpec as P

NCOEF = 55
NSAMP = 60


damping = 1.0


def slot_ranks(owner, parts):
    marks = (owner[:, None] == jnp.arange(parts, dtype=jnp.int32)[None, :]).astype(jnp.int32)
    running = jnp.cumsum(marks, axis=0) - 1
    return jnp.sum(running * marks, axis=1)


def block_sources(counts, first_block, nblocks):
    cum = jnp.cumsum(counts)
    index = first_block + jnp.arange(nblocks, dtype=jnp.int32)
    return jnp.sum((cum[None, :] <= index[:, None]).astype(jnp.int32), axis=1)


def unpack(block):
    spec = block[:, :NSAMP]
    coef = block[:, NSAMP : NSAMP + NCOEF]
    weight = block[:, NSAMP + NCOEF].astype(jnp.float32)
    unit = block[:, NSAMP + NCOEF + 1].astype(jnp.int32)
    return (spec, coef, weight, unit)


def unit_table(unit, units):
    return unit[:, None] == jnp.arange(units, dtype=jnp.int32)[None, :]


def update(base, moment, diag):
    shaped = moment.reshape(-1, NSAMP, NCOEF) / (diag[:, None, :] + damping)
    return base.astype(jnp.float32) + shaped.reshape(-1, NSAMP * NCOEF)


def body(coeffs, spectra, epoch_weight, source_blocks, epoch_owner, epoch_unit_local, design):
    parts = lax.axis_size("unit")
    myself = lax.axis_index("unit")
    epochs = spectra.shape[0]
    cap = epochs // 4
    nblocks = epochs // 128
    nsrc = coeffs.shape[0]
    units = design.shape[0]
    counts = source_blocks[0]
    block_src = block_sources(counts, myself * nblocks, nblocks)
    block_pick = (block_src[:, None] == jnp.arange(nsrc, dtype=jnp.int32)[None, :]).astype(
        jnp.float32
    )
    coef_blocks = jnp.dot(
        block_pick, coeffs, precision=lax.Precision.HIGHEST, preferred_element_type=jnp.float32
    ).astype(jnp.bfloat16)
    coef_epoch = jnp.repeat(coef_blocks, 128, axis=0)
    owner = epoch_owner[:, 0]
    rank = slot_ranks(owner, parts)
    slots = parts * cap
    filler = jnp.zeros((epochs, 128 - NSAMP - NCOEF - 2), jnp.bfloat16)
    items = jnp.concatenate(
        [
            spectra,
            coef_epoch,
            epoch_weight[:, None],
            epoch_unit_local[:, None].astype(jnp.bfloat16),
            filler,
        ],
        axis=1,
    )
    target = owner * cap + rank
    placer = (target[:, None] == jnp.arange(slots, dtype=jnp.int32)[None, :]).astype(jnp.bfloat16)
    outgoing = jnp.dot(placer.T, items, preferred_element_type=jnp.float32).astype(jnp.bfloat16)
    arrived = lax.all_to_all(
        outgoing.reshape(parts, cap, 128), "unit", split_axis=0, concat_axis=0, tiled=True
    )
    width = min(512, slots)
    blocked = arrived.reshape(slots // width, width, 128)

    def accumulate(carry, block):
        spec, coef, weight, unit = unpack(block)
        table = unit_table(unit, units)
        table_lo = table.astype(jnp.bfloat16)
        maps = jnp.dot(table_lo, design, preferred_element_type=jnp.float32).astype(jnp.bfloat16)
        maps = maps.reshape(-1, NSAMP, NCOEF)
        pred = jnp.einsum("bmk,bk->bm", maps, coef, preferred_element_type=jnp.float32)
        weighted = (weight[:, None] * (spec.astype(jnp.float32) - pred)).astype(jnp.bfloat16)
        spread = table_lo[:, :, None] * weighted[:, None, :]
        moment = jnp.einsum(
            "bum,bk->umk", spread, coef, preferred_element_type=jnp.float32
        ).reshape(units, NSAMP * NCOEF)
        coef_wide = coef.astype(jnp.float32)
        diag = jnp.dot(
            table.astype(jnp.float32).T,
            weight[:, None] * coef_wide * coef_wide,
            precision=lax.Precision.HIGHEST,
            preferred_element_type=jnp.float32,
        )
        return ((carry[0] + moment, carry[1] + diag), None)

    init = (jnp.zeros((units, NSAMP * NCOEF), jnp.float32), jnp.zeros((units, NCOEF), jnp.float32))
    (moment, diag), _ = lax.scan(accumulate, init, blocked)
    moment, diag = lax.psum((moment, diag), "src")
    new_design = update(design, moment, diag)
    refined_flat = new_design.astype(jnp.bfloat16)
    refined_wide = refined_flat.astype(jnp.float32).reshape(units, NSAMP, NCOEF)
    colsq = jnp.sum(refined_wide * refined_wide, axis=1)

    def terms(block):
        spec, coef, weight, unit = unpack(block)
        table = unit_table(unit, units)
        local_map = jnp.dot(
            table.astype(jnp.bfloat16), refined_flat, preferred_element_type=jnp.float32
        ).astype(jnp.bfloat16)
        local_map = local_map.reshape(-1, NSAMP, NCOEF)
        pred = jnp.einsum("bmk,bk->bm", local_map, coef, preferred_element_type=jnp.float32)
        weighted = (weight[:, None] * (spec.astype(jnp.float32) - pred)).astype(jnp.bfloat16)
        gradient = jnp.einsum(
            "bmk,bm->bk", local_map, weighted, preferred_element_type=jnp.float32
        ).astype(jnp.bfloat16)
        unit_colsq = jnp.dot(
            table.astype(jnp.float32),
            colsq,
            precision=lax.Precision.HIGHEST,
            preferred_element_type=jnp.float32,
        )
        curvature = (weight[:, None] * unit_colsq).astype(jnp.bfloat16)
        padding = jnp.zeros((block.shape[0], 128 - 2 * NCOEF), jnp.bfloat16)
        return jnp.concatenate([gradient, curvature, padding], axis=1)

    per_slot = lax.map(terms, blocked).reshape(slots, 128)
    back = lax.all_to_all(
        per_slot.reshape(parts, cap, 128), "unit", split_axis=0, concat_axis=0, tiled=True
    )
    mine = jnp.dot(placer, back.reshape(slots, 128), preferred_element_type=jnp.float32)
    block_totals = jnp.sum(mine.reshape(nblocks, 128, 128), axis=1)
    partial_value = jnp.dot(
        block_pick.T,
        block_totals,
        precision=lax.Precision.HIGHEST,
        preferred_element_type=jnp.float32,
    )
    sums = lax.psum(partial_value, "unit")
    new_coeffs = coeffs + sums[:, :NCOEF] / (sums[:, NCOEF : 2 * NCOEF] + damping)
    return (new_design, new_coeffs)


def solution(mesh):
    return jax.shard_map(
        body,
        mesh=mesh,
        in_specs=(
            P("src", None),
            P(("src", "unit"), None),
            P(("src", "unit")),
            P("src", None),
            P(("src", "unit"), None),
            P(("src", "unit")),
            P("unit", None),
        ),
        out_specs=(P("unit", None), P("src", None)),
        check_vma=False,
    )
```

profile of v0, /device:TPU:1, one launch (start us, length us, event | category | flops | bytes accessed | tf_op | source)
XLA Modules:
  0.0 350.6 jit_solution(3420029892717866245)
XLA Ops:
  7.9 2.3 reduce-window.18
  15.7 1.3 concatenate.6
  17.0 2.3 fusion.22
  19.3 6.8 %all-to-all-start = ((bf16[8,256,128]{2,1,0:T(8,128)(2,1)}), bf16[8,256,128]{2,1,0:T(8,128)(2,1)S(1)}, u32[]{:S(2)}, u32[]{:S(2)}) async-start(bf16[8,256,128]{2,1,0:T(8,128)(2,1)} %bitcast.12), calls=%async_computation | async-start | bytes 1048576 | tf_op jit(solution)/shard_map/all_to_all | solution.py:76
  26.2 9.5 %all-to-all-done = bf16[8,256,128]{2,1,0:T(8,128)(2,1)S(1)} async-done(((bf16[8,256,128]{2,1,0:T(8,128)(2,1)}), bf16[8,256,128]{2,1,0:T(8,128)(2,1)S(1)}, u32[]{:S(2)}, u32[]{:S(2)}) %all-to-all-start) | async-done | bytes 524320 | tf_op jit(solution)/shard_map/all_to_all | solution.py:76
  35.6 1.0 copy.28
  36.6 101.7 %while.24 = (s32[]{:T(128)}, f32[256,3300]{0,1:T(8,128)}, f32[256,55]{0,1:T(8,128)S(1)}, bf16[4,512,128]{1,2,0:T(8,128)(2,1)}, bf16[256,3300]{0,1:T(8,128)(2,1)}, /*index=5*/s32[]{:T(128)}, s32[]{:T(128)}) while((s32[]{:T(128)}, f32[256,3300]{0,1:T(8,128)}, f32[256,55]{0,1:T(8,128)S(1)}, bf16[4,512,128]{1,2,0:T(8,128)(2,1)}, ...), condition=%wide.region_6.7_spmd.clone, body=%wide.region_5.6_spmd.clone.sunk | while | flops 1833728512 | bytes 38276240 | solution.py:104
  38.2 4.3 %convolution_convert_fusion.6 = bf16[512,3300]{0,1:T(8,128)(2,1)} fusion(bf16[256,3300]{0,1:T(8,128)(2,1)} %get-tuple-element.228, s32[512]{0:T(512)S(1)} %bitcast.98), kind=kOutput, calls=%fused_computation.21.clone.1 | convolution fusion | flops 866895872 | bytes 5070848 | tf_op jit(solution)/shard_map/while/body/eval_jaxpr/dot_general | solution.py:86
  42.5 3.1 reshape.159
  45.7 0.9 slice_convert_fusion.13
  46.6 1.0 multiply_reduce_fusion.8
  47.8 6.6 %fusion.60 = f32[256,60,55]{0,2,1:T(8,128)} fusion(bf16[512,60]{0,1:T(8,128)(2,1)S(1)} %multiply_convert_fusion.3, bf16[512,256]{1,0:T(8,128)(2,1)S(1)} %fusion.59, bf16[512,128]{0,1:T(8,128)(2,1)S(1)} %copy-done.3), kind=kOutput, calls=%fused_computation.16.clone.1 | convolution fusion | flops 872939520 | bytes 3764224 | tf_op jit(solution)/shard_map/while/body/eval_jaxpr/bum,bk->umk/dot_general | solution.py:91
  54.4 2.8 reshape.160
  57.2 2.2 select_add_fusion.2
  59.4 1.2 convolution_add_fusion.2
  62.2 4.3 %convolution_convert_fusion.6 = bf16[512,3300]{0,1:T(8,128)(2,1)} fusion(bf16[256,3300]{0,1:T(8,128)(2,1)} %get-tuple-element.228, s32[512]{0:T(512)S(1)} %bitcast.98), kind=kOutput, calls=%fused_computation.21.clone.1 | convolution fusion | flops 866895872 | bytes 5070848 | tf_op jit(solution)/shard_map/while/body/eval_jaxpr/dot_general | solution.py:86
  66.5 3.1 reshape.159
  70.6 1.0 multiply_reduce_fusion.8
  71.7 6.6 %fusion.60 = f32[256,60,55]{0,2,1:T(8,128)} fusion(bf16[512,60]{0,1:T(8,128)(2,1)S(1)} %multiply_convert_fusion.3, bf16[512,256]{1,0:T(8,128)(2,1)S(1)} %fusion.59, bf16[512,128]{0,1:T(8,128)(2,1)S(1)} %copy-done.3), kind=kOutput, calls=%fused_computation.16.clone.1 | convolution fusion | flops 872939520 | bytes 3764224 | tf_op jit(solution)/shard_map/while/body/eval_jaxpr/bum,bk->umk/dot_general | solution.py:91
  78.4 2.8 reshape.160
  81.2 4.1 %select_add_fusion.2 = f32[256,3300]{0,1:T(8,128)} fusion(f32[256,3300]{0,1:T(8,128)S(1)} %reshape.160, f32[256,3300]{0,1:T(8,128)} %get-tuple-element.218, pred[]{:T(512)S(6)} %compare.3), kind=kLoop, calls=%fused_computation.22.clone.1 | loop fusion | flops 1689600 | bytes 10137601 | tf_op jit(solution)/shard_map/while/body/eval_jaxpr/add | solution.py:101
  85.3 1.2 convolution_add_fusion.2
  88.1 4.3 %convolution_convert_fusion.6 = bf16[512,3300]{0,1:T(8,128)(2,1)} fusion(bf16[256,3300]{0,1:T(8,128)(2,1)} %get-tuple-element.228, s32[512]{0:T(512)S(1)} %bitcast.98), kind=kOutput, calls=%fused_computation.21.clone.1 | convolution fusion | flops 866895872 | bytes 5070848 | tf_op jit(solution)/shard_map/while/body/eval_jaxpr/dot_general | solution.py:86
  92.4 3.1 reshape.159
  95.6 0.9 slice_convert_fusion.13
  96.5 1.0 multiply_reduce_fusion.8
  97.7 6.6 %fusion.60 = f32[256,60,55]{0,2,1:T(8,128)} fusion(bf16[512,60]{0,1:T(8,128)(2,1)S(1)} %multiply_convert_fusion.3, bf16[512,256]{1,0:T(8,128)(2,1)S(1)} %fusion.59, bf16[512,128]{0,1:T(8,128)(2,1)S(1)} %copy-done.3), kind=kOutput, calls=%fused_computation.16.clone.1 | convolution fusion | flops 872939520 | bytes 3764224 | tf_op jit(solution)/shard_map/while/body/eval_jaxpr/bum,bk->umk/dot_general | solution.py:91
  104.3 2.8 reshape.160
  107.1 4.1 %select_add_fusion.2 = f32[256,3300]{0,1:T(8,128)} fusion(f32[256,3300]{0,1:T(8,128)S(1)} %reshape.160, f32[256,3300]{0,1:T(8,128)} %get-tuple-element.218, pred[]{:T(512)S(6)} %compare.3), kind=kLoop, calls=%fused_computation.22.clone.1 | loop fusion | flops 1689600 | bytes 10137601 | tf_op jit(solution)/shard_map/while/body/eval_jaxpr/add | solution.py:101
  111.2 1.2 convolution_add_fusion.2
  114.0 4.3 %convolution_convert_fusion.6 = bf16[512,3300]{0,1:T(8,128)(2,1)} fusion(bf16[256,3300]{0,1:T(8,128)(2,1)} %get-tuple-element.228, s32[512]{0:T(512)S(1)} %bitcast.98), kind=kOutput, calls=%fused_computation.21.clone.1 | convolution fusion | flops 866895872 | bytes 5070848 | tf_op jit(solution)/shard_map/while/body/eval_jaxpr/dot_general | solution.py:86
  118.4 3.1 reshape.159
  121.5 0.9 slice_convert_fusion.13
  122.4 1.0 multiply_reduce_fusion.8
  123.6 6.6 %fusion.60 = f32[256,60,55]{0,2,1:T(8,128)} fusion(bf16[512,60]{0,1:T(8,128)(2,1)S(1)} %multiply_convert_fusion.3, bf16[512,256]{1,0:T(8,128)(2,1)S(1)} %fusion.59, bf16[512,128]{0,1:T(8,128)(2,1)S(1)} %copy-done.3), kind=kOutput, calls=%fused_computation.16.clone.1 | convolution fusion | flops 872939520 | bytes 3764224 | tf_op jit(solution)/shard_map/while/body/eval_jaxpr/bum,bk->umk/dot_general | solution.py:91
  130.2 2.8 reshape.160
  133.0 4.1 %select_add_fusion.2 = f32[256,3300]{0,1:T(8,128)} fusion(f32[256,3300]{0,1:T(8,128)S(1)} %reshape.160, f32[256,3300]{0,1:T(8,128)} %get-tuple-element.218, pred[]{:T(512)S(6)} %compare.3), kind=kLoop, calls=%fused_computation.22.clone.1 | loop fusion | flops 1689600 | bytes 10137601 | tf_op jit(solution)/shard_map/while/body/eval_jaxpr/add | solution.py:101
  137.1 1.2 convolution_add_fusion.2
  138.4 61.4 %psum.22 = f32[256,55]{0,1:T(8,128)S(1)} all-reduce(f32[256,55]{0,1:T(8,128)S(1)} %get-tuple-element.58), channel_id=1, replica_groups=mesh['src'=16,'unit'=8] {'src'}, use_global_device_ids=true, to_apply=%region_8.9 | all-reduce | flops 14080 | bytes 112640 | tf_op jit(solution)/shard_map/psum | solution.py:105
  200.0 2.2 div.15
  202.2 32.8 %all-reduce.2.cloned.1.call-done = f32[256,3300]{0,1:T(8,128)} async-done(((f32[256,3300]{0,1:T(8,128)}), f32[256,3300]{0,1:T(8,128)}) %all-reduce.2.cloned.1.call-update) | async-done | bytes 3379216 | tf_op jit(solution)/shard_map/psum | solution.py:105
  235.0 7.6 %convert_multiply_fusion = (f32[256,3300]{0,1:T(8,128)}, bf16[256,3300]{0,1:T(8,128)(2,1)}, f32[256,3300]{0,1:T(8,128)}) fusion(f32[256,3300]{0,1:T(8,128)} %all-reduce.2.cloned.1.call-done, f32[256,3300]{0,1:T(8,128)} %div.15, bf16[256,3300]{0,1:T(8,128)(2,1)} %param.17), kind=kLoop, calls=%fused_computation.45 | loop fusion | flops 5068800 | bytes 16896000 | tf_op jit(solution)/shard_map/mul | solution.py:109
  242.6 2.8 mul.82
  246.3 3.8 %copy.30 = bf16[256,3300]{1,0:T(8,128)(2,1)} copy(bf16[256,3300]{0,1:T(8,128)(2,1)} %get-tuple-element.134) | data formatting | bytes 3379200 | tf_op jit(solution)/shard_map/while | solution.py:133
  250.1 53.7 %while.23 = (s32[]{:T(128)}, bf16[4,512,128]{2,1,0:T(8,128)(2,1)}, bf16[4,512,128]{1,2,0:T(8,128)(2,1)}, bf16[256,3300]{1,0:T(8,128)(2,1)}, f32[256,55]{1,0:T(8,128)}, /*index=5*/s32[]{:T(128)}, bf16[]{:T(256)}, bf16[]{:T(256)}) while((s32[]{:T(128)}, bf16[4,512,128]{2,1,0:T(8,128)(2,1)}, bf16[4,512,128]{1,2,0:T(8,128)(2,1)}, ...), condition=%wide.region_11.12_spmd, body=%wide.region_10.11_spmd.sunk | while | flops 964245504 | bytes 21908728 | solution.py:133
  251.7 4.4 %convolution_convert_fusion.5 = bf16[512,3300]{0,1:T(8,128)(2,1)} fusion(bf16[256,3300]{1,0:T(8,128)(2,1)} %get-tuple-element.250, s32[512]{0:T(512)S(1)} %bitcast.102), kind=kOutput, calls=%fused_computation.2.clone.1 | convolution fusion | flops 866895872 | bytes 5070848 | tf_op jit(solution)/shard_map/while/body/eval_jaxpr/dot_general | solution.py:114
  256.1 3.1 reshape.158
  260.2 1.0 multiply_reduce_fusion.6
  261.2 0.9 multiply_reduce_fusion.7
  265.1 4.4 %convolution_convert_fusion.5 = bf16[512,3300]{0,1:T(8,128)(2,1)} fusion(bf16[256,3300]{1,0:T(8,128)(2,1)} %get-tuple-element.250, s32[512]{0:T(512)S(1)} %bitcast.102), kind=kOutput, calls=%fused_computation.2.clone.1 | convolution fusion | flops 866895872 | bytes 5070848 | tf_op jit(solution)/shard_map/while/body/eval_jaxpr/dot_general | solution.py:114
  269.6 3.1 reshape.158
  273.7 1.0 multiply_reduce_fusion.6
  274.7 0.9 multiply_reduce_fusion.7
  278.6 4.4 %convolution_convert_fusion.5 = bf16[512,3300]{0,1:T(8,128)(2,1)} fusion(bf16[256,3300]{1,0:T(8,128)(2,1)} %get-tuple-element.250, s32[512]{0:T(512)S(1)} %bitcast.102), kind=kOutput, calls=%fused_computation.2.clone.1 | convolution fusion | flops 866895872 | bytes 5070848 | tf_op jit(solution)/shard_map/while/body/eval_jaxpr/dot_general | solution.py:114
  283.0 3.1 reshape.158
  287.1 1.0 multiply_reduce_fusion.6
  288.1 0.9 multiply_reduce_fusion.7
  292.0 4.4 %convolution_convert_fusion.5 = bf16[512,3300]{0,1:T(8,128)(2,1)} fusion(bf16[256,3300]{1,0:T(8,128)(2,1)} %get-tuple-element.250, s32[512]{0:T(512)S(1)} %bitcast.102), kind=kOutput, calls=%fused_computation.2.clone.1 | convolution fusion | flops 866895872 | bytes 5070848 | tf_op jit(solution)/shard_map/while/body/eval_jaxpr/dot_general | solution.py:114
  296.4 3.1 reshape.158
  300.5 1.0 multiply_reduce_fusion.6
  301.5 0.9 multiply_reduce_fusion.7
  303.9 14.9 %all_to_all.10 = bf16[8,256,128]{2,1,0:T(8,128)(2,1)S(1)} all-to-all(bf16[8,256,128]{2,1,0:T(8,128)(2,1)} %bitcast.104), channel_id=1, replica_groups=mesh['src'=16,'unit'=8] {'unit'}, dimensions={0} | all-to-all | bytes 1048576 | tf_op jit(solution)/shard_map/all_to_all | solution.py:134
  318.8 2.8 fusion.25
  321.9 21.2 %psum.23 = f32[24,128]{1,0:T(8,128)S(1)} all-reduce(f32[24,128]{1,0:T(8,128)S(1)} %fusion.33), channel_id=1, replica_groups=mesh['src'=16,'unit'=8] {'unit'}, use_global_device_ids=true, to_apply=%region_13.14 | all-reduce | flops 3072 | bytes 24576 | tf_op jit(solution)/shard_map/psum | solution.py:145
  (130 shorter events, 31.9 us)
Async XLA Ops:
  19.3 16.3 %all-to-all-start = ((bf16[8,256,128]{2,1,0:T(8,128)(2,1)}), bf16[8,256,128]{2,1,0:T(8,128)(2,1)S(1)}, u32[]{:S(2)}, u32[]{:S(2)}) async-start(bf16[8,256,128]{2,1,0:T(8,128)(2,1)} %bitcast.12), calls=%async_computation | async-start | bytes 1048576 | tf_op jit(solution)/shard_map/all_to_all | solution.py:76
  26.2 208.8 %all-reduce.2.cloned.1.call-start = ((), (), s32[]{:S(2)}) async-start(), calls=%async_computation.2 | async-start | bytes 6766592 | tf_op jit(solution)/shard_map/psum | solution.py:105
  37.6 0.7 copy-start.2
  45.7 1.9 copy-start.3
  61.5 0.7 copy-start.2
  69.7 1.9 copy-start.3
  87.4 0.7 copy-start.2
  95.6 1.9 copy-start.3
  113.4 0.7 copy-start.2
  121.5 1.9 copy-start.3
  251.1 0.6 copy-start
  259.3 1.9 copy-start.1
  260.2 1.9 copy-start.4
  264.5 0.6 copy-start
  272.7 1.9 copy-start.1
  273.7 1.9 copy-start.4
  277.9 0.6 copy-start
  286.1 1.9 copy-start.1
  287.1 1.9 copy-start.4
  291.3 0.6 copy-start
  299.6 1.9 copy-start.1
  300.5 1.9 copy-start.4
  303.9 39.2 %copy-start.5 = (f32[24,55]{1,0:T(8,128)S(1)}, f32[24,55]{1,0:T(8,128)}, u32[]{:S(2)}) copy-start(f32[24,55]{1,0:T(8,128)} %param.11) | copy-start | bytes 15844
Sparse Core Ops, SparseCore 0:
  138.5 96.4 all-reduce.1
where the time goes:
time: 355 us; the launch traced here: 351 us
  blocking collectives  97.4 us (27%)
  matrix products  74.4 us (21%)
  local copies, waits for them, and re-layouts  66.2 us (19%)
  other arithmetic  48.6 us (14%)
  waiting for transfers between devices  42.3 us (12%)
  between operations  14.1 us (4%)
  starting transfers between devices  6.82 us (2%)
    psum x1, blocking collectives, body(): moment, diag = lax.psum((moment, diag), 'src')  61.4 us
    psum x1, waiting for transfers between devices, body(): moment, diag = lax.psum((moment, diag), 'src')  32.8 us
    dot_general x4, matrix products, accumulate(): jnp.einsum('bum,bk->umk', spread, coef, preferred_element_type=jnp.float32)  26.5 us
    psum x1, blocking collectives, body(): sums = lax.psum(partial_value, 'unit')  21.2 us
    dot_general x4, matrix products, terms(): jnp.dot(table.astype(jnp.bfloat16), refined_flat, preferred_element_type=...  17.7 us
    dot_general x4, matrix products, accumulate(): jnp.dot(table_lo, design, preferred_element_type=jnp.float32)  17.3 us
    all_to_all x1, blocking collectives, body(): lax.all_to_all(per_slot.reshape(parts, cap, 128), 'unit', split_axis=0, c...  14.9 us
    add x4, other arithmetic, accumulate(): return ((carry[0] + moment, carry[1] + diag), None)  14.6 us
  transfers between devices with their start and end apart: 2, of which 2 were waited for; matrix products, arithmetic and copies ran while one was open for 1% of the time, Pallas kernels for 0%

commit v1 on v0

v1 whole, which is shorter than its diff:
```python
import functools

import jax
import jax.numpy as jnp
from jax import lax
from jax.experimental import pallas as pl
from jax.experimental.pallas import tpu as pltpu
from jax.sharding import PartitionSpec as P

NCOEF = 55
NSAMP = 60
HALF = 64
LANES = 128
BLOCK = 128
GROUP = 16
damping = 1.0

MESH = pl.DeviceIdType.MESH
BF = jnp.bfloat16
F32 = jnp.float32


def dot(a, b):
    return jnp.dot(a, b, preferred_element_type=F32)


def dot_nt(a, b):
    return lax.dot_general(a, b, (((1,), (1,)), ((), ())), preferred_element_type=F32)


def dot_tn(a, b):
    return lax.dot_general(a, b, (((0,), (0,)), ((), ())), preferred_element_type=F32)


def iota(shape, dim):
    return lax.broadcasted_iota(jnp.int32, shape, dim)


def ones_where(mask):
    return jnp.where(mask, 1.0, 0.0).astype(BF)


def kernel(
    n_src,
    n_unit,
    nsrc,
    spec_ref,
    w_ref,
    u_ref,
    o_ref,
    cnt_ref,
    coef_ref,
    design_ref,
    gath_ref,
    nc_ref,
    dbuf,
    rank_ref,
    items_ref,
    place_ref,
    out1,
    recv1,
    acc_ref,
    xbuf,
    sbuf,
    recv2,
    sf_ref,
    cp_ref,
    fbuf,
    d2t,
    wb_ref,
    s2_ref,
    flat_ref,
    gh_ref,
    recv3,
    g1_ref,
    recv4,
    dsem,
    ssem1,
    rsem1,
    ssem2,
    rsem2,
    ssem3,
    rsem3,
    ssem4,
    rsem4,
    ssem5,
    rsem5,
):
    row = lax.axis_index("src")
    me = lax.axis_index("unit")
    epochs = spec_ref.shape[0]
    nblocks = epochs // BLOCK
    units = n_src * GROUP
    pairs = nsrc // 2
    half_slots = LANES
    width = pairs * LANES
    wide = GROUP * LANES
    rows_t = n_src * GROUP

    def unit_at(i):
        return lax.rem(me + i, n_unit)

    def row_at(i):
        return lax.rem(row + i, n_src)

    barrier = pltpu.get_barrier_semaphore()
    for i in range(1, n_unit):
        pl.semaphore_signal(barrier, inc=1, device_id={"unit": unit_at(i)}, device_id_type=MESH)
    for i in range(1, n_src):
        pl.semaphore_signal(barrier, inc=1, device_id={"src": row_at(i)}, device_id_type=MESH)

    load = pltpu.make_async_copy(
        design_ref.at[pl.ds(pl.multiple_of(row * GROUP, GROUP), GROUP)], dbuf, dsem
    )
    load.start()

    owner = o_ref[...]
    marks = jnp.concatenate(
        [jnp.where(owner == j, 1.0, 0.0) for j in range(n_unit)], axis=0
    )
    marks_lo = marks.astype(BF)
    earlier = ones_where(iota((LANES, LANES), 0) < iota((LANES, LANES), 1))
    inside = dot(marks_lo, earlier)
    totals = dot(marks_lo, jnp.ones((LANES, LANES), BF)).astype(BF)
    nrow = n_unit * nblocks
    a, b = iota((nrow, nrow), 0), iota((nrow, nrow), 1)
    before = ones_where((a // nblocks == b // nblocks) & (b < a))
    rank_ref[...] = jnp.where(marks > 0.0, inside + dot(before, totals), -1.0)

    count = jnp.broadcast_to(cnt_ref[...].astype(F32), (nblocks, nsrc)).astype(BF)
    upto = ones_where(iota((nsrc, LANES), 0) <= iota((nsrc, LANES), 1))
    cum = dot(count, upto)
    index = (me * nblocks + iota((nblocks, LANES), 0)).astype(F32)
    done = ones_where((cum <= index) & (iota((nblocks, LANES), 1) < nsrc))
    source = dot(done, jnp.ones((LANES, LANES), BF))
    meta = jnp.concatenate(
        [w_ref[...].astype(F32), u_ref[...].astype(F32), source], axis=0
    ).astype(BF)
    sub, lane = iota((NSAMP, 2 * LANES), 0), iota((NSAMP, 2 * LANES), 1)
    spread = ones_where((lane == sub) | (lane == sub + LANES + HALF))
    sub, lane = iota((3 * nblocks, 2 * LANES), 0), iota((3 * nblocks, 2 * LANES), 1)
    for block in range(nblocks):
        rows = slice(block * BLOCK, (block + 1) * BLOCK)
        pick = jnp.zeros(sub.shape, jnp.bool_)
        for field, at in enumerate((62, 63, 61)):
            here = (lane == at) | (lane == LANES + HALF + at)
            pick = pick | (here & (sub == field * nblocks + block))
        both = dot(spec_ref[rows, :], spread) + dot_tn(meta, ones_where(pick))
        both = both.astype(BF)
        items_ref[rows, :] = both[:, :LANES]
        items_ref[epochs + block * BLOCK : epochs + (block + 1) * BLOCK, :] = both[:, LANES:]

    slot = iota((LANES, LANES), 0).astype(F32)
    for i in range(n_unit):
        ranks = rank_ref[pl.ds(pl.multiple_of(unit_at(i) * nblocks, nblocks), nblocks), :]
        for block in range(nblocks):
            line = jnp.broadcast_to(ranks[block : block + 1, :], (LANES, LANES))
            at = slice(i * LANES, (i + 1) * LANES)
            place_ref[at, block * BLOCK : (block + 1) * BLOCK] = ones_where(line == slot)
            place_ref[at, epochs + block * BLOCK : epochs + (block + 1) * BLOCK] = ones_where(
                line == slot + float(half_slots)
            )
    packed = dot(place_ref[...], items_ref[...]).astype(BF)
    for i in range(n_unit):
        out1[i] = packed[i * LANES : (i + 1) * LANES]

    pl.semaphore_wait(barrier, n_unit + n_src - 2)
    sends1 = []
    for i in range(1, n_unit):
        copy = pltpu.make_async_remote_copy(
            src_ref=out1.at[i],
            dst_ref=recv1.at[i],
            send_sem=ssem1.at[i],
            recv_sem=rsem1.at[i],
            device_id={"unit": unit_at(i)},
            device_id_type=MESH,
        )
        copy.start()
        sends1.append(copy)

    coef_lo = coef_ref[...].astype(BF)
    at_row, at_src = iota((GROUP, nsrc), 0), iota((GROUP, nsrc), 1)
    k_row, k_lane = iota((NCOEF, LANES), 0), iota((NCOEF, LANES), 1)
    cp_own = jnp.zeros((GROUP, LANES), F32)
    for par in range(2):
        rows = ones_where((at_src == at_row + par * pairs) & (at_row < pairs))
        taken = dot(rows, coef_lo).astype(BF)
        cp_own = cp_own + dot(taken, ones_where(k_lane == k_row + par * HALF))
    cp_own = cp_own.astype(BF)

    load.wait()
    fbuf[...] = jnp.zeros_like(fbuf)
    own = dbuf[...].astype(F32)
    for m in range(NSAMP):
        fbuf[m * GROUP : (m + 1) * GROUP, 0:NCOEF] = own[:, m * NCOEF : (m + 1) * NCOEF]
    for u in range(GROUP):
        one = fbuf[pl.ds(u, HALF, stride=GROUP), :]
        twice = jnp.concatenate([one, one], axis=0)
        d2t[:, u * LANES : (u + 1) * LANES] = twice.T[:HALF]

    sub, lane = iota((LANES, 4 * LANES), 0), iota((LANES, 4 * LANES), 1)
    part, within = lane // LANES, lane % LANES
    data = (part < 2) & (sub == part * HALF + within % HALF) & (within % HALF < NSAMP)
    expand = ones_where(data | ((part >= 2) & (sub == (part - 2) * HALF + 61)))
    within = iota((LANES, LANES), 1) % HALF
    shift = jnp.where(iota((LANES, LANES), 1) >= HALF, float(pairs), 0.0)
    unit_row = iota((units, LANES), 0).astype(F32)
    for i in range(n_unit):
        if i == 0:
            got = out1[0]
        else:
            sends1[i - 1].wait_recv()
            got = recv1[i]
        spread4 = dot(got, expand)
        turned = got.astype(F32).T
        table = []
        for side in range(2):
            wrow = jnp.broadcast_to(turned[side * HALF + 62 : side * HALF + 63], (units, LANES))
            urow = jnp.broadcast_to(turned[side * HALF + 63 : side * HALF + 64], (units, LANES))
            table.append(jnp.where(unit_row == urow, wrow, 0.0).astype(BF))
            values = spread4[:, side * LANES : (side + 1) * LANES]
            values = jnp.where(within >= NSAMP, 1.0, values)
            which = spread4[:, (2 + side) * LANES : (3 + side) * LANES] - shift
            for t in range(pairs):
                xbuf[side * LANES : (side + 1) * LANES, t * LANES : (t + 1) * LANES] = jnp.where(
                    which == float(t), values, 0.0
                ).astype(BF)
        part_sum = dot(jnp.concatenate(table, axis=1), xbuf[...])
        if i == 0:
            acc_ref[...] = part_sum
        else:
            acc_ref[...] += part_sum

    low_lane = iota((GROUP, width), 1) % HALF == 61
    for g in range(n_src):
        rows = slice(g * GROUP, (g + 1) * GROUP)
        total = acc_ref[rows, :]
        high = total.astype(BF)
        rest = total - high.astype(F32)
        sbuf[rows, 0:width] = jnp.where(low_lane, rest, high.astype(F32)).astype(BF)
        sbuf[rows, width : width + LANES] = cp_own

    sends2 = []
    for i in range(1, n_src):
        copy = pltpu.make_async_remote_copy(
            src_ref=sbuf.at[pl.ds(pl.multiple_of(row_at(i) * GROUP, GROUP), GROUP)],
            dst_ref=recv2.at[i],
            send_sem=ssem2.at[i],
            recv_sem=rsem2.at[i],
            device_id={"src": row_at(i)},
            device_id_type=MESH,
        )
        copy.start()
        sends2.append(copy)

    for i in range(n_src):
        if i == 0:
            got = sbuf[pl.ds(pl.multiple_of(row * GROUP, GROUP), GROUP), :]
            origin = row
        else:
            sends2[i - 1].wait_recv()
            got = recv2[i]
            origin = row_at(n_src - i)
        for t in range(GROUP):
            start = pl.multiple_of((origin * GROUP + t) * GROUP, GROUP)
            if t < pairs:
                sf_ref[pl.ds(start, GROUP), :] = got[:, t * LANES : (t + 1) * LANES].astype(F32)
            else:
                sf_ref[pl.ds(start, GROUP), :] = jnp.zeros((GROUP, LANES), F32)
        cp_ref[pl.ds(pl.multiple_of(origin * GROUP, GROUP), GROUP), :] = got[:, width:]

    sub, lane = iota((LANES, 2 * LANES), 0), iota((LANES, 2 * LANES), 1) % LANES
    kind = iota((LANES, 2 * LANES), 1) // LANES
    bring = ones_where(sub == (lane // HALF) * HALF + NSAMP + kind)
    for u in range(GROUP):
        lanes = slice(u * LANES, (u + 1) * LANES)
        tile = sf_ref[pl.ds(u, rows_t, stride=GROUP), :].astype(BF)
        s2_ref[:, lanes] = tile
        weights = dot(tile, bring)
        wb_ref[0, :, lanes] = weights[:, :LANES].astype(BF)
        wb_ref[1, :, lanes] = weights[:, LANES:].astype(BF)
    cp = cp_ref[...]
    cp_wide = cp.astype(F32)
    cpt = cp_wide.T
    cpt_lo = cpt.astype(BF)
    sq = cpt * cpt
    sq_hi = sq.astype(BF)
    sq_lo = (sq - sq_hi.astype(F32)).astype(BF)
    lane = iota((HALF, wide), 1)
    first = lane % LANES < HALF
    real = lane % HALF < NSAMP

    def two_halves(x):
        return jnp.concatenate(
            [jnp.where(first, x, 0.0), jnp.where(first, 0.0, x)], axis=0
        ).astype(BF)

    def fold(x):
        y = jnp.where(first, x[:HALF], x[HALF:])
        return jnp.concatenate(
            [
                y[:, u * LANES : (u + 1) * LANES]
                + pltpu.roll(y[:, u * LANES : (u + 1) * LANES], HALF, 1)
                for u in range(GROUP)
            ],
            axis=1,
        )

    sums = s2_ref[...].astype(F32)
    weight = wb_ref[0].astype(F32) + wb_ref[1].astype(F32)
    base = d2t[...]
    resid = (sums - weight * dot(cp, two_halves(base))).astype(BF)
    moment = fold(dot(cpt_lo, resid))
    diag = fold(dot(sq_hi, wb_ref[0]) + dot(sq_lo, wb_ref[0]) + dot(sq_hi, wb_ref[1]))
    refined = jnp.where(real, base + moment / (diag + damping), 0.0).astype(BF)
    refined_wide = refined.astype(F32)
    maps = two_halves(refined_wide)
    resid = (sums - weight * dot(cp, maps)).astype(BF)
    square = refined_wide * refined_wide
    square_hi = square.astype(BF)
    square_lo = (square - square_hi.astype(F32)).astype(BF)
    firsts = ones_where(iota((LANES, LANES), 0) < HALF)
    colsq = jnp.concatenate(
        [
            dot(square_hi[:, u * LANES : (u + 1) * LANES], firsts)
            + dot(square_lo[:, u * LANES : (u + 1) * LANES], firsts)
            for u in range(GROUP)
        ],
        axis=1,
    )
    colsq_hi = colsq.astype(BF).astype(F32)
    place = lane % HALF
    curve = jnp.where((place == 60) | (place == 61), colsq_hi, 0.0)
    curve = jnp.where(place == 62, colsq - colsq_hi, curve)
    both = jnp.concatenate([maps, two_halves(curve)], axis=0)
    gh_ref[...] = dot_nt(resid, both)

    sends3 = []
    for i in range(1, n_src):
        copy = pltpu.make_async_remote_copy(
            src_ref=gh_ref.at[pl.ds(pl.multiple_of(row_at(i) * GROUP, GROUP), GROUP)],
            dst_ref=recv3.at[i],
            send_sem=ssem3.at[i],
            recv_sem=rsem3.at[i],
            device_id={"src": row_at(i)},
            device_id_type=MESH,
        )
        copy.start()
        sends3.append(copy)

    maps_wide = maps.astype(F32)
    for u in range(GROUP):
        turned = maps_wide[:, u * LANES : (u + 1) * LANES].T
        fbuf[pl.ds(u, HALF, stride=GROUP), :] = turned[:HALF]
    pieces = [fbuf[m * GROUP : (m + 1) * GROUP, 0:NCOEF] for m in range(NSAMP)]
    filler = jnp.zeros((GROUP, flat_ref.shape[1] - NSAMP * NCOEF), F32)
    flat_ref[...] = jnp.concatenate(pieces + [filler], axis=1).astype(BF)
    mine = pl.ds(pl.multiple_of(row * GROUP, GROUP), GROUP)
    keep = pltpu.make_async_copy(flat_ref, gath_ref.at[mine], dsem)
    keep.start()
    sends5 = []
    for i in range(1, n_src):
        copy = pltpu.make_async_remote_copy(
            src_ref=flat_ref,
            dst_ref=gath_ref.at[mine],
            send_sem=ssem5.at[i],
            recv_sem=rsem5.at[i],
            device_id={"src": row_at(i)},
            device_id_type=MESH,
        )
        copy.start()
        sends5.append(copy)

    total = gh_ref[pl.ds(pl.multiple_of(row * GROUP, GROUP), GROUP), :]
    for i in range(1, n_src):
        sends3[i - 1].wait_recv()
        total = total + recv3[i]
    g1_ref[...] = total
    sends4 = []
    for i in range(1, n_unit):
        copy = pltpu.make_async_remote_copy(
            src_ref=g1_ref,
            dst_ref=recv4.at[me],
            send_sem=ssem4.at[i],
            recv_sem=rsem4.at[i],
            device_id={"unit": unit_at(i)},
            device_id_type=MESH,
        )
        copy.start()
        sends4.append(copy)
    recv4[me] = total
    for copy in sends4:
        copy.wait_recv()
    total = recv4[0]
    for j in range(1, n_unit):
        total = total + recv4[j]
    step = total[:, :LANES] / (total[:, LANES:] + damping)
    other = pltpu.roll(step, HALF, 1)
    coef = coef_ref[...]
    nc_ref[0:pairs, :] = coef[0:pairs] + step[0:pairs, 0:NCOEF]
    nc_ref[pairs:nsrc, :] = coef[pairs:nsrc] + other[0:pairs, 0:NCOEF]

    keep.wait()
    for copy in sends5:
        copy.wait_recv()
    for copy in sends1 + sends2 + sends3 + sends4 + sends5:
        copy.wait_send()


def body(coeffs, spectra, epoch_weight, source_blocks, epoch_owner, epoch_unit_local, design):
    n_src = lax.axis_size("src")
    n_unit = lax.axis_size("unit")
    epochs = spectra.shape[0]
    nblocks = epochs // BLOCK
    nsrc = coeffs.shape[0]
    units, flat = design.shape
    padded = -(-flat // LANES) * LANES
    width = (nsrc // 2) * LANES
    rows_t = n_src * GROUP
    wide = GROUP * LANES
    vmem = pl.BlockSpec(memory_space=pltpu.VMEM)
    any_space = pl.BlockSpec(memory_space=pl.ANY)
    sems = pltpu.SemaphoreType.DMA
    gathered, new_coeffs = pl.pallas_call(
        functools.partial(kernel, n_src, n_unit, nsrc),
        out_shape=(
            jax.ShapeDtypeStruct((units, padded), BF),
            jax.ShapeDtypeStruct(coeffs.shape, F32),
        ),
        in_specs=[vmem] * 6 + [any_space],
        out_specs=(any_space, vmem),
        scratch_shapes=[
            pltpu.VMEM((GROUP, flat), BF),
            pltpu.VMEM((n_unit * nblocks, LANES), F32),
            pltpu.VMEM((2 * epochs, LANES), BF),
            pltpu.VMEM((n_unit * LANES, 2 * epochs), BF),
            pltpu.VMEM((n_unit, LANES, LANES), BF),
            pltpu.VMEM((n_unit, LANES, LANES), BF),
            pltpu.VMEM((units, width), F32),
            pltpu.VMEM((2 * LANES, width), BF),
            pltpu.VMEM((units, width + LANES), BF),
            pltpu.VMEM((n_src, GROUP, width + LANES), BF),
            pltpu.VMEM((rows_t * GROUP, LANES), F32),
            pltpu.VMEM((rows_t, LANES), BF),
            pltpu.VMEM((HALF * GROUP, LANES), F32),
            pltpu.VMEM((HALF, wide), F32),
            pltpu.VMEM((2, rows_t, wide), BF),
            pltpu.VMEM((rows_t, wide), BF),
            pltpu.VMEM((GROUP, padded), BF),
            pltpu.VMEM((rows_t, 2 * LANES), F32),
            pltpu.VMEM((n_src, GROUP, 2 * LANES), F32),
            pltpu.VMEM((GROUP, 2 * LANES), F32),
            pltpu.VMEM((n_unit, GROUP, 2 * LANES), F32),
            sems,
            sems((n_unit,)),
            sems((n_unit,)),
            sems((n_src,)),
            sems((n_src,)),
            sems((n_src,)),
            sems((n_src,)),
            sems((n_unit,)),
            sems((n_unit,)),
            sems((n_src,)),
            sems((n_src,)),
        ],
        compiler_params=pltpu.CompilerParams(
            collective_id=0, has_side_effects=True, vmem_limit_bytes=48 * 1024 * 1024
        ),
    )(
        spectra,
        epoch_weight.reshape(nblocks, BLOCK),
        epoch_unit_local.reshape(nblocks, BLOCK),
        epoch_owner.reshape(nblocks, BLOCK),
        source_blocks,
        coeffs,
        design,
    )
    return (gathered[:, :flat].astype(F32), new_coeffs)


def solution(mesh):
    return jax.shard_map(
        body,
        mesh=mesh,
        in_specs=(
            P("src", None),
            P(("src", "unit"), None),
            P(("src", "unit")),
            P("src", None),
            P(("src", "unit"), None),
            P(("src", "unit")),
            P("unit", None),
        ),
        out_specs=(P("unit", None), P("src", None)),
        check_vma=False,
    )
```

time: 355 us -> 72.6 us (0.20)
  the two profiles are of different devices: /device:TPU:1 before, /device:TPU:28 now
where the time goes in v1:
time: 72.6 us; the launch traced here: 72.4 us
  Pallas kernels  64 us (88%)
  local copies, waits for them, and re-layouts  7.41 us (10%)
  between operations  0.74 us (1%)
    pallas_call x1, Pallas kernels, body(): pl.pallas_call(functools.partial(kernel, n_src, n_unit, nsrc), out_shape=...  64 us
    unnamed x14, local copies, waits for them, and re-layouts  7.41 us

profile of v1, /device:TPU:28, one launch (start us, length us, event | category | flops | bytes accessed | tf_op | source)
XLA Modules:
  0.0 72.4 jit_solution(8405431623581614407)
XLA Ops:
  0.6 1.1 %copy.9.spec_ref = bf16[1024,60]{1,0:T(8,128)(2,1)S(1)} copy(bf16[1024,60]{0,1:T(8,128)(2,1)} %param.8) | data formatting | bytes 245760 | tf_op args[1]
  1.7 0.0 copy-start
  1.7 0.0 copy-start.1
  1.7 0.0 copy-start.2
  1.8 0.0 copy-start.3
  1.8 0.0 copy-start.4
  1.8 2.8 %copy.10.design_ref = bf16[256,3300]{1,0:T(8,128)(2,1)S(1)} copy(bf16[256,3300]{0,1:T(8,128)(2,1)} %param.13) | data formatting | bytes 3379200 | tf_op args[6]
  4.5 0.0 copy-done
  4.5 0.0 copy-done.1
  4.6 0.0 copy-done.2
  4.6 0.0 copy-done.3
  4.6 0.0 copy-done.4
  4.6 64.0 %shard_map.86 = (bf16[256,3328]{1,0:T(8,128)(2,1)S(1)}, f32[24,55]{1,0:T(8,128)S(1)}) custom-call(bf16[1024,60]{1,0:T(8,128)(2,1)S(1)} %copy.9.spec_ref, bf16[8,128]{1,0:T(8,128)(2,1)S(1)} %bitcast.5, s32[8,128]{1,0:T(8,128)S(1)} %bitcast.3, s32[8,128]{1,0:T(8,128)S(1)} %bitcast.4, s32[1,24]{1,0:T(1,128)S(1)} %copy-done.4, f32[24,55]{1,0:T(8,128)S(1)} %copy-done, ...), custom_call_target="tpu_custom_call" | custom-call | tf_op jit(solution)/shard_map/pallas_call | solution.py:424
  68.6 0.2 slice_convert_fusion
  68.9 2.9 %copy.11 = f32[256,3300]{0,1:T(8,128)} copy(f32[256,3300]{1,0:T(8,128)S(1)} %slice_convert_fusion) | data formatting | bytes 6758400
  71.8 0.6 copy.13
Async XLA Ops:
  1.7 2.8 %copy-start = (f32[24,55]{1,0:T(8,128)S(1)}, f32[24,55]{1,0:T(8,128)}, u32[]{:S(2)}) copy-start(f32[24,55]{1,0:T(8,128)} %coef_ref.1) | copy-start | bytes 15844
  1.7 2.8 %copy-start.1 = (s32[1024]{0:T(1024)S(1)}, s32[1024]{0:T(1024)}, u32[]{:S(2)}) copy-start(s32[1024]{0:T(1024)} %param.12) | copy-start | bytes 12292
  1.7 2.8 %copy-start.2 = (s32[1024,1]{0,1:T(1,128)S(1)}, s32[1024,1]{0,1:T(1,128)}, u32[]{:S(2)}) copy-start(s32[1024,1]{0,1:T(1,128)} %param.11) | copy-start | bytes 12292
  1.8 2.8 %copy-start.3 = (bf16[1024]{0:T(1024)(128)(2,1)S(1)}, bf16[1024]{0:T(1024)(128)(2,1)}, u32[]{:S(2)}) copy-start(bf16[1024]{0:T(1024)(128)(2,1)} %param.9) | copy-start | bytes 6148
  1.8 2.8 %copy-start.4 = (s32[1,24]{1,0:T(1,128)S(1)}, s32[1,24]{1,0:T(1,128)}, u32[]{:S(2)}) copy-start(s32[1,24]{1,0:T(1,128)} %cnt_ref.1) | copy-start | bytes 292

commit v2 on v1

--- a/solution.py
+++ b/solution.py
@@ -59,6 +59,7 @@
     place_ref,
     out1,
     recv1,
+    table_ref,
     acc_ref,
     xbuf,
     sbuf,
@@ -88,11 +89,11 @@
 ):
     row = lax.axis_index("src")
     me = lax.axis_index("unit")
-    epochs = spec_ref.shape[0]
+    epochs = spec_ref.shape[1]
     nblocks = epochs // BLOCK
     units = n_src * GROUP
     pairs = nsrc // 2
-    half_slots = LANES
+    slots = place_ref.shape[1]
     width = pairs * LANES
     wide = GROUP * LANES
     rows_t = n_src * GROUP
@@ -109,9 +110,7 @@
     for i in range(1, n_src):
         pl.semaphore_signal(barrier, inc=1, device_id={"src": row_at(i)}, device_id_type=MESH)
 
-    load = pltpu.make_async_copy(
-        design_ref.at[pl.ds(pl.multiple_of(row * GROUP, GROUP), GROUP)], dbuf, dsem
-    )
+    load = pltpu.make_async_copy(design_ref, dbuf, dsem)
     load.start()
 
     owner = o_ref[...]
@@ -133,50 +132,39 @@
     index = (me * nblocks + iota((nblocks, LANES), 0)).astype(F32)
     done = ones_where((cum <= index) & (iota((nblocks, LANES), 1) < nsrc))
     source = dot(done, jnp.ones((LANES, LANES), BF))
-    meta = jnp.concatenate(
-        [w_ref[...].astype(F32), u_ref[...].astype(F32), source], axis=0
+    weights, locals_ = w_ref[...].astype(F32), u_ref[...].astype(F32)
+
+    def one_row(x):
+        return jnp.concatenate([x[b : b + 1, :] for b in range(nblocks)], axis=1)
+
+    spare = jnp.zeros((HALF - NSAMP - 3, epochs), F32)
+    items_ref[0:48, :] = spec_ref[0:48, :]
+    items_ref[48:64, :] = jnp.concatenate(
+        [spec_ref[48:NSAMP, :].astype(F32), one_row(weights), one_row(locals_), one_row(source), spare],
+        axis=0,
     ).astype(BF)
-    sub, lane = iota((NSAMP, 2 * LANES), 0), iota((NSAMP, 2 * LANES), 1)
-    spread = ones_where((lane == sub) | (lane == sub + LANES + HALF))
-    sub, lane = iota((3 * nblocks, 2 * LANES), 0), iota((3 * nblocks, 2 * LANES), 1)
-    for block in range(nblocks):
-        rows = slice(block * BLOCK, (block + 1) * BLOCK)
-        pick = jnp.zeros(sub.shape, jnp.bool_)
-        for field, at in enumerate((62, 63, 61)):
-            here = (lane == at) | (lane == LANES + HALF + at)
-            pick = pick | (here & (sub == field * nblocks + block))
-        both = dot(spec_ref[rows, :], spread) + dot_tn(meta, ones_where(pick))
-        both = both.astype(BF)
-        items_ref[rows, :] = both[:, :LANES]
-        items_ref[epochs + block * BLOCK : epochs + (block + 1) * BLOCK, :] = both[:, LANES:]
-
-    slot = iota((LANES, LANES), 0).astype(F32)
-    for i in range(n_unit):
+
+    pl.semaphore_wait(barrier, n_unit + n_src - 2)
+    slot = iota((slots, LANES), 0).astype(F32)
+    sends1 = []
+    for k in range(n_unit):
+        i = (k + 1) % n_unit
         ranks = rank_ref[pl.ds(pl.multiple_of(unit_at(i) * nblocks, nblocks), nblocks), :]
         for block in range(nblocks):
-            line = jnp.broadcast_to(ranks[block : block + 1, :], (LANES, LANES))
-            at = slice(i * LANES, (i + 1) * LANES)
-            place_ref[at, block * BLOCK : (block + 1) * BLOCK] = ones_where(line == slot)
-            place_ref[at, epochs + block * BLOCK : epochs + (block + 1) * BLOCK] = ones_where(
-                line == slot + float(half_slots)
+            line = jnp.broadcast_to(ranks[block : block + 1, :], (slots, LANES))
+            place_ref[i, :, block * BLOCK : (block + 1) * BLOCK] = ones_where(line == slot)
+        out1[i] = dot_nt(items_ref[...], place_ref[i]).astype(BF)
+        if i > 0:
+            copy = pltpu.make_async_remote_copy(
+                src_ref=out1.at[i],
+                dst_ref=recv1.at[i],
+                send_sem=ssem1.at[i],
+                recv_sem=rsem1.at[i],
+                device_id={"unit": unit_at(i)},
+                device_id_type=MESH,
             )
-    packed = dot(place_ref[...], items_ref[...]).astype(BF)
-    for i in range(n_unit):
-        out1[i] = packed[i * LANES : (i + 1) * LANES]
-
-    pl.semaphore_wait(barrier, n_unit + n_src - 2)
-    sends1 = []
-    for i in range(1, n_unit):
-        copy = pltpu.make_async_remote_copy(
-            src_ref=out1.at[i],
-            dst_ref=recv1.at[i],
-            send_sem=ssem1.at[i],
-            recv_sem=rsem1.at[i],
-            device_id={"unit": unit_at(i)},
-            device_id_type=MESH,
-        )
-        copy.start()
-        sends1.append(copy)
+            copy.start()
+            sends1.append(copy)
 
     coef_lo = coef_ref[...].astype(BF)
     at_row, at_src = iota((GROUP, nsrc), 0), iota((GROUP, nsrc), 1)
@@ -190,7 +178,8 @@
 
     load.wait()
     fbuf[...] = jnp.zeros_like(fbuf)
-    own = dbuf[...].astype(F32)
+    at_own, at_unit = iota((GROUP, units), 0), iota((GROUP, units), 1)
+    own = dot_nt(ones_where(at_unit == at_own + row * GROUP), dbuf[...])
     for m in range(NSAMP):
         fbuf[m * GROUP : (m + 1) * GROUP, 0:NCOEF] = own[:, m * NCOEF : (m + 1) * NCOEF]
     for u in range(GROUP):
@@ -198,35 +187,31 @@
         twice = jnp.concatenate([one, one], axis=0)
         d2t[:, u * LANES : (u + 1) * LANES] = twice.T[:HALF]
 
-    sub, lane = iota((LANES, 4 * LANES), 0), iota((LANES, 4 * LANES), 1)
-    part, within = lane // LANES, lane % LANES
-    data = (part < 2) & (sub == part * HALF + within % HALF) & (within % HALF < NSAMP)
-    expand = ones_where(data | ((part >= 2) & (sub == (part - 2) * HALF + 61)))
-    within = iota((LANES, LANES), 1) % HALF
-    shift = jnp.where(iota((LANES, LANES), 1) >= HALF, float(pairs), 0.0)
-    unit_row = iota((units, LANES), 0).astype(F32)
-    for i in range(n_unit):
-        if i == 0:
-            got = out1[0]
-        else:
-            sends1[i - 1].wait_recv()
-            got = recv1[i]
-        spread4 = dot(got, expand)
-        turned = got.astype(F32).T
-        table = []
-        for side in range(2):
-            wrow = jnp.broadcast_to(turned[side * HALF + 62 : side * HALF + 63], (units, LANES))
-            urow = jnp.broadcast_to(turned[side * HALF + 63 : side * HALF + 64], (units, LANES))
-            table.append(jnp.where(unit_row == urow, wrow, 0.0).astype(BF))
-            values = spread4[:, side * LANES : (side + 1) * LANES]
-            values = jnp.where(within >= NSAMP, 1.0, values)
-            which = spread4[:, (2 + side) * LANES : (3 + side) * LANES] - shift
+    unit_row = iota((units, slots), 0).astype(F32)
+    field = iota((HALF, slots), 0)
+    group = 4
+    for first in range(0, n_unit, group):
+        for part in range(group):
+            i = first + part
+            if i == 0:
+                got = out1[0]
+            else:
+                sends1[i - 1].wait_recv()
+                got = recv1[i]
+            got = got.astype(F32)
+            at = slice(part * slots, (part + 1) * slots)
+            wrow = jnp.broadcast_to(got[60:61], (units, slots))
+            urow = jnp.broadcast_to(got[61:62], (units, slots))
+            table_ref[:, at] = jnp.where(unit_row == urow, wrow, 0.0).astype(BF)
+            srow = jnp.broadcast_to(got[62:63], (HALF, slots))
+            values = jnp.where(field < NSAMP, got, 1.0)
             for t in range(pairs):
-                xbuf[side * LANES : (side + 1) * LANES, t * LANES : (t + 1) * LANES] = jnp.where(
-                    which == float(t), values, 0.0
-                ).astype(BF)
-        part_sum = dot(jnp.concatenate(table, axis=1), xbuf[...])
-        if i == 0:
+                for par in range(2):
+                    here = slice(t * LANES + par * HALF, t * LANES + par * HALF + HALF)
+                    keep = srow == float(t + par * pairs)
+                    xbuf[here, at] = jnp.where(keep, values, 0.0).astype(BF)
+        part_sum = dot_nt(table_ref[...], xbuf[...])
+        if first == 0:
             acc_ref[...] = part_sum
         else:
             acc_ref[...] += part_sum
@@ -407,6 +392,23 @@
         copy.wait_send()
 
 
+def turn_kernel(in_ref, out_ref):
+    n = out_ref.shape[0]
+    same = ones_where(iota((n, n), 0) == iota((n, n), 1))
+    out_ref[...] = dot_nt(same, in_ref[...])
+
+
+def turn(x, rows):
+    units, step = x.shape[0], 2 * LANES
+    return pl.pallas_call(
+        turn_kernel,
+        out_shape=jax.ShapeDtypeStruct((rows, units), F32),
+        grid=(-(-rows // step),),
+        in_specs=[pl.BlockSpec((units, step), lambda i: (0, i))],
+        out_specs=pl.BlockSpec((step, units), lambda i: (i, 0)),
+    )(x)
+
+
 def body(coeffs, spectra, epoch_weight, source_blocks, epoch_owner, epoch_unit_local, design):
     n_src = lax.axis_size("src")
     n_unit = lax.axis_size("unit")
@@ -418,6 +420,7 @@
     width = (nsrc // 2) * LANES
     rows_t = n_src * GROUP
     wide = GROUP * LANES
+    slots = epochs // 4
     vmem = pl.BlockSpec(memory_space=pltpu.VMEM)
     any_space = pl.BlockSpec(memory_space=pl.ANY)
     sems = pltpu.SemaphoreType.DMA
@@ -430,14 +433,15 @@
         in_specs=[vmem] * 6 + [any_space],
         out_specs=(any_space, vmem),
         scratch_shapes=[
-            pltpu.VMEM((GROUP, flat), BF),
+            pltpu.VMEM((flat, units), BF),
             pltpu.VMEM((n_unit * nblocks, LANES), F32),
-            pltpu.VMEM((2 * epochs, LANES), BF),
-            pltpu.VMEM((n_unit * LANES, 2 * epochs), BF),
-            pltpu.VMEM((n_unit, LANES, LANES), BF),
-            pltpu.VMEM((n_unit, LANES, LANES), BF),
+            pltpu.VMEM((HALF, epochs), BF),
+            pltpu.VMEM((n_unit, slots, epochs), BF),
+            pltpu.VMEM((n_unit, HALF, slots), BF),
+            pltpu.VMEM((n_unit, HALF, slots), BF),
+            pltpu.VMEM((units, 4 * slots), BF),
             pltpu.VMEM((units, width), F32),
-            pltpu.VMEM((2 * LANES, width), BF),
+            pltpu.VMEM((width, 4 * slots), BF),
             pltpu.VMEM((units, width + LANES), BF),
             pltpu.VMEM((n_src, GROUP, width + LANES), BF),
             pltpu.VMEM((rows_t * GROUP, LANES), F32),
@@ -467,15 +471,15 @@
             collective_id=0, has_side_effects=True, vmem_limit_bytes=48 * 1024 * 1024
         ),
     )(
-        spectra,
+        spectra.T,
         epoch_weight.reshape(nblocks, BLOCK),
         epoch_unit_local.reshape(nblocks, BLOCK),
         epoch_owner.reshape(nblocks, BLOCK),
         source_blocks,
         coeffs,
-        design,
+        design.T,
     )
-    return (gathered[:, :flat].astype(F32), new_coeffs)
+    return (turn(gathered, flat).T, new_coeffs)
 
 
 def solution(mesh):

time: 72.6 us -> 80.2 us (1.10)
  the two profiles are of different devices: /device:TPU:28 before, /device:TPU:24 now
where the time goes in v2:
time: 80.2 us; the launch traced here: 79.7 us
  Pallas kernels  71.4 us (89%)
  local copies, waits for them, and re-layouts  7.57 us (9%)
    pallas_call x1, Pallas kernels, body(): pl.pallas_call(functools.partial(kernel, n_src, n_unit, nsrc), out_shape=...  62.1 us
    pallas_call x1, Pallas kernels, turn(): pl.pallas_call(turn_kernel, out_shape=jax.ShapeDtypeStruct((rows, units),...  9.31 us
    unnamed x17, local copies, waits for them, and re-layouts  7.57 us

profile of v2, /device:TPU:24, one launch (start us, length us, event | category | flops | bytes accessed | tf_op | source)
XLA Modules:
  0.0 79.7 jit_solution(13085760814522775537)
XLA Ops:
  0.6 0.0 copy-start.1
  0.6 1.4 %copy-done.1 = bf16[256,3300]{0,1:T(8,128)(2,1)S(1)} copy-done((bf16[256,3300]{0,1:T(8,128)(2,1)S(1)}, bf16[256,3300]{0,1:T(8,128)(2,1)}, u32[]{:S(2)}) %copy-start.1) | copy-done | bytes 1689624
  2.1 0.0 copy-start.2
  2.1 0.9 %copy-done.2 = bf16[1024,60]{0,1:T(8,128)(2,1)S(1)} copy-done((bf16[1024,60]{0,1:T(8,128)(2,1)S(1)}, bf16[1024,60]{0,1:T(8,128)(2,1)}, u32[]{:S(2)}) %copy-start.2) | copy-done | bytes 122904
  3.0 0.0 copy-start.3
  3.0 0.7 copy-done.3
  3.7 0.0 copy-start.4
  3.7 0.7 copy-done.4
  4.4 0.0 copy-start.5
  4.4 0.7 copy-done.5
  5.1 0.0 copy-start.6
  5.1 0.7 copy-done.6
  5.8 0.0 copy-start.7
  5.8 0.7 copy-done.7
  6.4 62.1 %shard_map.86 = (bf16[256,3328]{1,0:T(8,128)(2,1)S(1)}, f32[24,55]{1,0:T(8,128)S(1)}) custom-call(bf16[60,1024]{1,0:T(8,128)(2,1)S(1)} %bitcast.7, bf16[8,128]{1,0:T(8,128)(2,1)S(1)} %bitcast.10, s32[8,128]{1,0:T(8,128)S(1)} %bitcast.8, s32[8,128]{1,0:T(8,128)S(1)} %bitcast.9, s32[1,24]{1,0:T(1,128)S(1)} %copy-done.7, f32[24,55]{1,0:T(8,128)S(1)} %copy-done.3, ...), custom_call_target="tpu_custom_call" | custom-call | tf_op jit(solution)/shard_map/pallas_call | solution.py:427
  68.5 0.0 copy-start
  68.5 1.2 %copy-done = bf16[256,3328]{1,0:T(8,128)(2,1)} copy-done((bf16[256,3328]{1,0:T(8,128)(2,1)}, bf16[256,3328]{1,0:T(8,128)(2,1)S(1)}, u32[]{:S(2)}) %copy-start) | copy-done | bytes 1703960
  69.8 9.3 %shard_map.87 = f32[3300,256]{1,0:T(8,128)} custom-call(bf16[256,3328]{1,0:T(8,128)(2,1)} %copy-done), custom_call_target="tpu_custom_call" | custom-call | tf_op jit(solution)/shard_map/pallas_call | solution.py:403
  79.1 0.6 copy.10
Async XLA Ops:
  0.6 1.5 %copy-start.1 = (bf16[256,3300]{0,1:T(8,128)(2,1)S(1)}, bf16[256,3300]{0,1:T(8,128)(2,1)}, u32[]{:S(2)}) copy-start(bf16[256,3300]{0,1:T(8,128)(2,1)} %param.13) | copy-start | bytes 5068804
  2.1 0.9 %copy-start.2 = (bf16[1024,60]{0,1:T(8,128)(2,1)S(1)}, bf16[1024,60]{0,1:T(8,128)(2,1)}, u32[]{:S(2)}) copy-start(bf16[1024,60]{0,1:T(8,128)(2,1)} %param.8) | copy-start | bytes 368644
  3.0 0.7 copy-start.3
  3.7 0.7 copy-start.4
  4.4 0.7 copy-start.5
  5.1 0.7 copy-start.6
  5.8 0.7 copy-start.7
  68.5 1.2 %copy-start = (bf16[256,3328]{1,0:T(8,128)(2,1)}, bf16[256,3328]{1,0:T(8,128)(2,1)S(1)}, u32[]{:S(2)}) copy-start(bf16[256,3328]{1,0:T(8,128)(2,1)S(1)} %get-tuple-element.4.in_ref) | copy-start | bytes 5111812

commit v3 on v0

v3 whole, which is shorter than its diff:
```python
import functools
import math

import jax
import jax.numpy as jnp
from jax import lax
from jax.experimental import pallas as pl
from jax.experimental.pallas import tpu as pltpu
from jax.sharding import PartitionSpec as P

NCOEF = 55
NSAMP = 60
HALF = 64
LANES = 128
BLOCK = 128
SLOTS = 256
damping = 1.0

MESH = pl.DeviceIdType.MESH
BF = jnp.bfloat16
F32 = jnp.float32


def dot(a, b):
    return jnp.dot(a, b, preferred_element_type=F32)


def dot_nt(a, b):
    return lax.dot_general(a, b, (((1,), (1,)), ((), ())), preferred_element_type=F32)


def iota(shape, dim):
    return lax.broadcasted_iota(jnp.int32, shape, dim)


def ones_where(mask):
    return jnp.where(mask, 1.0, 0.0).astype(BF)


def split(x):
    high = x.astype(BF)
    return high, (x - high.astype(F32)).astype(BF)


def up(x, n):
    return -(-x // n) * n


def kernel(
    n_src,
    n_unit,
    nsrc,
    spec_hbm,
    w_hbm,
    u_hbm,
    o_hbm,
    cnt_hbm,
    coef_hbm,
    design_hbm,
    out_ref,
    nc_ref,
    spec_ref,
    w_ref,
    u_ref,
    o_ref,
    cnt_ref,
    coef_ref,
    dbuf,
    rank_ref,
    items_ref,
    place_ref,
    out1,
    recv1,
    cown,
    crecv,
    c_ref,
    dk_ref,
    table_ref,
    mark_ref,
    xbuf,
    sbuf,
    recv2,
    sf_ref,
    w2_ref,
    wlow_ref,
    emap,
    eflat,
    gbuf,
    gh_ref,
    csq_ref,
    recv3,
    g1_ref,
    recv4,
    lsem,
    csem,
    crsem,
    ssem1,
    rsem1,
    ssem2,
    rsem2,
    ssem3,
    rsem3,
    ssem4,
    rsem4,
    ssem5,
    ssem6,
    rsem5,
):
    row = lax.axis_index("src")
    me = lax.axis_index("unit")
    epochs = spec_ref.shape[1]
    nblocks = epochs // BLOCK
    units = 2 * LANES
    groups = n_src // 2
    samples = HALF // groups
    part_rows = samples * nsrc
    all_src = n_src * nsrc
    side = math.isqrt(n_src)
    flat = dbuf.shape[0]
    owner_rows = samples * NCOEF
    half_rows = eflat.shape[0] // 2
    my_half, my_group = row // groups, row % groups

    def unit_at(i):
        return lax.rem(me + i, n_unit)

    def row_at(i):
        return lax.rem(row + i, n_src)

    def loop(lo, hi):
        return pl.loop(lo, hi)

    barrier = pltpu.get_barrier_semaphore()

    @loop(1, n_unit)
    def _(i):
        pl.semaphore_signal(barrier, inc=1, device_id={"unit": unit_at(i)}, device_id_type=MESH)

    @loop(1, n_src)
    def _(i):
        pl.semaphore_signal(barrier, inc=1, device_id={"src": row_at(i)}, device_id_type=MESH)

    loads = [
        pltpu.make_async_copy(a, b, lsem.at[n])
        for n, (a, b) in enumerate(
            [
                (o_hbm, o_ref),
                (cnt_hbm, cnt_ref),
                (w_hbm, w_ref),
                (u_hbm, u_ref),
                (spec_hbm, spec_ref),
                (coef_hbm, coef_ref),
                (design_hbm, dbuf),
            ]
        )
    ]
    for load in loads:
        load.start()
    for load in loads[:-1]:
        load.wait()

    owner = o_ref[...]
    marks = jnp.concatenate([jnp.where(owner == j, 1.0, 0.0) for j in range(n_unit)], axis=0)
    marks_lo = marks.astype(BF)
    earlier = ones_where(iota((LANES, LANES), 0) < iota((LANES, LANES), 1))
    inside = dot(marks_lo, earlier)
    totals = dot(marks_lo, jnp.ones((LANES, LANES), BF)).astype(BF)
    nrow = n_unit * nblocks
    a, b = iota((nrow, nrow), 0), iota((nrow, nrow), 1)
    before = ones_where((a // nblocks == b // nblocks) & (b < a))
    rank_ref[...] = jnp.where(marks > 0.0, inside + dot(before, totals), -1.0)

    count = jnp.broadcast_to(cnt_ref[...].astype(F32), (nblocks, nsrc)).astype(BF)
    upto = ones_where(iota((nsrc, LANES), 0) <= iota((nsrc, LANES), 1))
    cum = dot(count, upto)
    index = (me * nblocks + iota((nblocks, LANES), 0)).astype(F32)
    done = ones_where((cum <= index) & (iota((nblocks, LANES), 1) < nsrc))
    source = dot(done, jnp.ones((LANES, LANES), BF))
    weights, locals_ = w_ref[...].astype(F32), u_ref[...].astype(F32)

    def one_row(x):
        return jnp.concatenate([x[b : b + 1, :] for b in range(nblocks)], axis=1)

    spare = jnp.zeros((HALF - NSAMP - 3, epochs), F32)
    items_ref[0:48, :] = spec_ref[0:48, :]
    items_ref[48:64, :] = jnp.concatenate(
        [
            spec_ref[48:NSAMP, :].astype(F32),
            one_row(weights),
            one_row(locals_),
            one_row(source),
            spare,
        ],
        axis=0,
    ).astype(BF)

    coef_lo = coef_ref[...].astype(BF)
    widen = ones_where(iota((NCOEF, LANES), 0) == iota((NCOEF, LANES), 1))
    deepen = ones_where(iota((cown.shape[0], nsrc), 0) == iota((cown.shape[0], nsrc), 1))
    padded = dot(deepen, dot(coef_lo, widen).astype(BF)).astype(BF)
    cown[...] = padded
    crecv[row] = padded

    pl.semaphore_wait(barrier, n_unit + n_src - 2)

    def send1(i):
        return pltpu.make_async_remote_copy(
            src_ref=out1.at[i],
            dst_ref=recv1.at[i],
            send_sem=ssem1.at[i],
            recv_sem=rsem1.at[i],
            device_id={"unit": unit_at(i)},
            device_id_type=MESH,
        )

    def send_coef(i):
        return pltpu.make_async_remote_copy(
            src_ref=cown,
            dst_ref=crecv.at[row],
            send_sem=csem.at[i],
            recv_sem=crsem.at[i],
            device_id={"src": row_at(i)},
            device_id_type=MESH,
        )

    slot = iota((SLOTS, LANES), 0).astype(F32)

    @loop(0, n_unit)
    def _(k):
        i = lax.rem(k + 1, n_unit)
        ranks = rank_ref[pl.ds(pl.multiple_of(unit_at(i) * nblocks, nblocks), nblocks), :]
        for block in range(nblocks):
            line = jnp.broadcast_to(ranks[block : block + 1, :], (SLOTS, LANES))
            place_ref[:, block * BLOCK : (block + 1) * BLOCK] = ones_where(line == slot)
        result = dot_nt(items_ref[...], place_ref[...]).astype(BF)
        out1[i] = result

        @pl.when(i > 0)
        def _():
            send1(i).start()

    @loop(1, n_src)
    def _(i):
        send_coef(i).start()

    loads[-1].wait()
    window = up(owner_rows + 15, 16)
    first_row = my_group * owner_rows
    start = jnp.minimum(first_row // 16 * 16, (flat - window) // 16 * 16)
    tail = flat // 16 * 16
    lanes_half = pl.ds(pl.multiple_of(my_half * LANES, LANES), LANES)
    shape = (samples * HALF, window)
    want = iota(shape, 0) // HALF * NCOEF + iota(shape, 0) % HALF + first_row
    real = iota(shape, 0) % HALF < NCOEF
    pick = ones_where(real & (want == iota(shape, 1) + start))
    maps = dot(pick, dbuf[pl.ds(pl.multiple_of(start, 16), window), lanes_half])
    shape = (samples * HALF, flat - tail)
    want = iota(shape, 0) // HALF * NCOEF + iota(shape, 0) % HALF + first_row
    real = iota(shape, 0) % HALF < NCOEF
    late = iota(shape, 1) + tail
    pick = ones_where(real & (want == late) & (late >= start + window))
    dk_ref[...] = maps + dot(pick, dbuf[tail:flat, lanes_half])

    unit_row = iota((units, SLOTS), 0).astype(F32)
    field = iota((HALF, SLOTS), 0)
    source_row = iota((mark_ref.shape[0], SLOTS), 0).astype(F32)
    recv1[0] = out1[0]

    @loop(0, n_unit)
    def _(i):
        @pl.when(i > 0)
        def _():
            send1(i).wait_recv()

        got = recv1[i].astype(F32)
        at = pl.ds(pl.multiple_of(i * SLOTS, SLOTS), SLOTS)
        wrow = jnp.broadcast_to(got[60:61], (units, SLOTS))
        urow = jnp.broadcast_to(got[61:62], (units, SLOTS))
        srow = got[62:63]
        table_ref[:, at] = jnp.where(unit_row == urow, wrow, 0.0).astype(BF)
        mark_ref[:, at] = ones_where(jnp.broadcast_to(srow, source_row.shape) == source_row)
        values = jnp.where(field < NSAMP, got, 0.0)
        srow = jnp.broadcast_to(srow, (samples, SLOTS))
        for s in range(0, nsrc, 2):
            one, two = srow == float(s), srow == float(s + 1)
            for g in range(groups):
                data = values[g * samples : (g + 1) * samples]
                both = jnp.concatenate([jnp.where(one, data, 0.0), jnp.where(two, data, 0.0)], axis=0)
                base = g * part_rows + s * samples
                xbuf[base : base + 2 * samples, at] = both.astype(BF)

    high, low = split(dot_nt(mark_ref[...], table_ref[...])[:nsrc])
    pair = jnp.concatenate([high.astype(F32), low.astype(F32)], axis=0).astype(BF)

    def send2(other):
        return pltpu.make_async_remote_copy(
            src_ref=sbuf.at[other],
            dst_ref=recv2.at[row],
            send_sem=ssem2.at[other],
            recv_sem=rsem2.at[row],
            device_id={"src": other},
            device_id_type=MESH,
        )

    def came2(other):
        return pltpu.make_async_remote_copy(
            src_ref=sbuf.at[other],
            dst_ref=recv2.at[other],
            send_sem=ssem2.at[other],
            recv_sem=rsem2.at[other],
            device_id={"src": other},
            device_id_type=MESH,
        )

    @loop(0, groups)
    def _(k):
        group = lax.rem(my_group + 1 + k, groups)
        x = xbuf[pl.ds(pl.multiple_of(group * part_rows, part_rows), part_rows), :]
        sums = dot_nt(x, table_ref[...]).astype(BF)
        for half in range(2):
            other = half * groups + group
            lanes = slice(half * LANES, (half + 1) * LANES)
            sbuf[other, 0:part_rows, :] = sums[:, lanes]
            sbuf[other, part_rows : part_rows + 2 * nsrc, :] = pair[:, lanes]

            @pl.when(other != row)
            def _():
                send2(other).start()

    recv2[row] = sbuf[row]

    @loop(0, n_src)
    def _(i):
        @pl.when(i > 0)
        def _():
            send_coef(i).wait_recv()

    @loop(0, n_src)
    def _(r):
        at = pl.ds(pl.multiple_of(r * nsrc, 8), nsrc)
        c_ref[at, :] = crecv[r].astype(F32)[:nsrc]

    @loop(0, n_src)
    def _(i):
        r = row_at(i)

        @pl.when(i > 0)
        def _():
            came2(r).wait_recv()

        got = recv2[r].astype(F32)
        sf_ref[pl.ds(pl.multiple_of(r * part_rows, part_rows), part_rows), :] = got[:part_rows]
        at = pl.ds(pl.multiple_of(r * nsrc, 8), nsrc)
        w2_ref[at, :] = got[part_rows : part_rows + nsrc] + got[part_rows + nsrc :]

    coef = c_ref[...]
    turned = coef.T[:HALF]
    turned_lo = turned.astype(BF)
    square_hi, square_lo = split(turned * turned)
    coef_all = coef[:, :HALF].astype(BF)
    weight_hi, weight_lo = split(w2_ref[...])
    wlow_ref[0] = weight_hi
    wlow_ref[1] = weight_lo
    diag = dot(square_hi, weight_hi) + dot(square_lo, weight_hi) + dot(square_hi, weight_lo)
    scale = 1.0 / (diag + damping)

    for m in range(samples):
        base = dk_ref[m * HALF : (m + 1) * HALF, :]
        sums = sf_ref[pl.ds(m, all_src, stride=samples), :]
        resid = (sums - w2_ref[...] * dot(coef_all, base.astype(BF))).astype(BF)
        refined = (base + dot(turned_lo, resid) * scale).astype(BF).astype(F32)
        emap[m] = refined
        dk_ref[m * NCOEF : (m + 1) * NCOEF, :] = refined[:NCOEF]
    if owner_rows < eflat.shape[0]:
        dk_ref[owner_rows : eflat.shape[0], :] = jnp.zeros((eflat.shape[0] - owner_rows, LANES), F32)
    eflat[...] = dk_ref[0 : eflat.shape[0], :].astype(BF)

    px, py = row // side, row % side

    def peer(axis, d):
        if axis == 0:
            return lax.rem(px + d, side) * side + py
        return px * side + lax.rem(py + d, side)

    def piece(half):
        return pl.ds(half * half_rows, half_rows)

    def stage1(half, d):
        return pltpu.make_async_remote_copy(
            src_ref=eflat.at[piece(half)],
            dst_ref=gbuf.at[row, piece(half)],
            send_sem=ssem5.at[half, d],
            recv_sem=rsem5.at[half, row],
            device_id={"src": peer(half, d)},
            device_id_type=MESH,
        )

    def stage2(half, q, d):
        origin = peer(half, q)
        return pltpu.make_async_remote_copy(
            src_ref=gbuf.at[origin, piece(half)],
            dst_ref=gbuf.at[origin, piece(half)],
            send_sem=ssem6.at[half, q, d],
            recv_sem=rsem5.at[half, origin],
            device_id={"src": peer(1 - half, d)},
            device_id_type=MESH,
        )

    def came5(half, origin):
        return pltpu.make_async_remote_copy(
            src_ref=gbuf.at[origin, piece(half)],
            dst_ref=gbuf.at[origin, piece(half)],
            send_sem=ssem5.at[half, 0],
            recv_sem=rsem5.at[half, origin],
            device_id={"src": row_at(1)},
            device_id_type=MESH,
        )

    gbuf[row] = eflat[...]

    @loop(1, side)
    def _(d):
        for half in range(2):
            stage1(half, d).start()

    @loop(1, side)
    def _(d):
        for half in range(2):
            stage2(half, 0, d).start()

    gh_ref[...] = jnp.zeros_like(gh_ref)
    csq_ref[...] = jnp.zeros_like(csq_ref)
    blank = jnp.zeros((HALF, LANES), F32)
    for m in range(samples):
        refined = emap[m]
        sums = sf_ref[pl.ds(m, all_src, stride=samples), :]
        resid = (sums - w2_ref[...] * dot(coef_all, refined.astype(BF))).astype(BF)
        gh_ref[...] += dot_nt(resid, jnp.concatenate([refined, blank], axis=0).astype(BF))
        csq_ref[...] += refined * refined
    curve_hi, curve_lo = split(jnp.concatenate([blank, csq_ref[...]], axis=0))
    gh_ref[...] += (
        dot_nt(wlow_ref[0], curve_hi) + dot_nt(wlow_ref[0], curve_lo) + dot_nt(wlow_ref[1], curve_hi)
    )

    def send3(i):
        return pltpu.make_async_remote_copy(
            src_ref=gh_ref.at[pl.ds(pl.multiple_of(row_at(i) * nsrc, 8), nsrc)],
            dst_ref=recv3.at[i],
            send_sem=ssem3.at[i],
            recv_sem=rsem3.at[i],
            device_id={"src": row_at(i)},
            device_id_type=MESH,
        )

    @loop(1, n_src)
    def _(i):
        send3(i).start()

    @loop(1, side)
    def _(q):
        for half in range(2):
            came5(half, peer(half, q)).wait_recv()

            @loop(1, side)
            def _(d):
                stage2(half, q, d).start()

    g1_ref[...] = gh_ref[pl.ds(pl.multiple_of(row * nsrc, 8), nsrc), :]

    @loop(1, n_src)
    def _(i):
        send3(i).wait_recv()
        g1_ref[...] += recv3[i]

    def send4(i):
        return pltpu.make_async_remote_copy(
            src_ref=g1_ref,
            dst_ref=recv4.at[me],
            send_sem=ssem4.at[i],
            recv_sem=rsem4.at[i],
            device_id={"unit": unit_at(i)},
            device_id_type=MESH,
        )

    @loop(1, n_unit)
    def _(i):
        send4(i).start()

    recv4[me] = g1_ref[...]

    @loop(1, n_unit)
    def _(i):
        send4(i).wait_recv()

    total = recv4[0]
    for j in range(1, n_unit):
        total = total + recv4[j]
    step = total / (pltpu.roll(total, HALF, 1) + damping)
    nc_ref[...] = coef_ref[...] + step[:, :NCOEF]

    def arrive(other):
        for half in range(2):
            same = (other // side == px) if half == 1 else (other % side == py)

            @pl.when(jnp.logical_not(same))
            def _():
                came5(half, other).wait_recv()

    for half in range(2):
        lanes = slice(half * LANES, (half + 1) * LANES)

        @loop(0, groups - 1)
        def _(group):
            other = half * groups + group
            arrive(other)
            at = pl.ds(pl.multiple_of(group * owner_rows, 8), owner_rows)
            out_ref[at, lanes] = gbuf[other][:owner_rows]

        other = half * groups + groups - 1
        arrive(other)
        done_rows = (groups - 1) * owner_rows
        out_ref[done_rows:flat, lanes] = gbuf[other][: flat - done_rows]

    @loop(1, n_unit)
    def _(i):
        send1(i).wait_send()
        send4(i).wait_send()

    @loop(1, n_src)
    def _(i):
        send_coef(i).wait_send()
        send2(row_at(i)).wait_send()
        send3(i).wait_send()

    @loop(1, side)
    def _(d):
        for half in range(2):
            stage1(half, d).wait_send()
            for q in range(side):
                stage2(half, q, d).wait_send()


def body(coeffs, spectra, epoch_weight, source_blocks, epoch_owner, epoch_unit_local, design):
    n_src = lax.axis_size("src")
    n_unit = lax.axis_size("unit")
    epochs = spectra.shape[0]
    nblocks = epochs // BLOCK
    nsrc = coeffs.shape[0]
    units, flat = design.shape
    groups = n_src // 2
    samples = HALF // groups
    part_rows = samples * nsrc
    message = part_rows + 2 * nsrc
    all_src = n_src * nsrc
    side = math.isqrt(n_src)
    erows = up(samples * NCOEF, 32)
    vmem = pl.BlockSpec(memory_space=pltpu.VMEM)
    hbm = pl.BlockSpec(memory_space=pltpu.HBM)
    sems = pltpu.SemaphoreType.DMA
    new_design, new_coeffs = pl.pallas_call(
        functools.partial(kernel, n_src, n_unit, nsrc),
        out_shape=(
            jax.ShapeDtypeStruct((flat, units), BF),
            jax.ShapeDtypeStruct(coeffs.shape, F32),
        ),
        in_specs=[hbm] * 7,
        out_specs=(vmem, vmem),
        scratch_shapes=[
            pltpu.VMEM((NSAMP, epochs), BF),
            pltpu.VMEM((nblocks, BLOCK), BF),
            pltpu.VMEM((nblocks, BLOCK), jnp.int32),
            pltpu.VMEM((nblocks, BLOCK), jnp.int32),
            pltpu.VMEM((1, nsrc), jnp.int32),
            pltpu.VMEM(coeffs.shape, F32),
            pltpu.VMEM((flat, units), BF),
            pltpu.VMEM((n_unit * nblocks, LANES), F32),
            pltpu.VMEM((HALF, epochs), BF),
            pltpu.VMEM((SLOTS, epochs), BF),
            pltpu.VMEM((n_unit, HALF, SLOTS), BF),
            pltpu.VMEM((n_unit, HALF, SLOTS), BF),
            pltpu.VMEM((up(nsrc, 16), LANES), BF),
            pltpu.VMEM((n_src, up(nsrc, 16), LANES), BF),
            pltpu.VMEM((all_src, LANES), F32),
            pltpu.VMEM((samples * HALF, LANES), F32),
            pltpu.VMEM((units, n_unit * SLOTS), BF),
            pltpu.VMEM((up(nsrc, 16), n_unit * SLOTS), BF),
            pltpu.VMEM((groups * part_rows, n_unit * SLOTS), BF),
            pltpu.VMEM((n_src, message, LANES), BF),
            pltpu.VMEM((n_src, message, LANES), BF),
            pltpu.VMEM((n_src * part_rows, LANES), F32),
            pltpu.VMEM((all_src, LANES), F32),
            pltpu.VMEM((2, all_src, LANES), BF),
            pltpu.VMEM((samples, HALF, LANES), F32),
            pltpu.VMEM((erows, LANES), BF),
            pltpu.VMEM((n_src, erows, LANES), BF),
            pltpu.VMEM((all_src, LANES), F32),
            pltpu.VMEM((HALF, LANES), F32),
            pltpu.VMEM((n_src, nsrc, LANES), F32),
            pltpu.VMEM((nsrc, LANES), F32),
            pltpu.VMEM((n_unit, nsrc, LANES), F32),
            sems((7,)),
            sems((n_src,)),
            sems((n_src,)),
            sems((n_unit,)),
            sems((n_unit,)),
            sems((n_src,)),
            sems((n_src,)),
            sems((n_src,)),
            sems((n_src,)),
            sems((n_unit,)),
            sems((n_unit,)),
            sems((2, side)),
            sems((2, side, side)),
            sems((2, n_src)),
        ],
        compiler_params=pltpu.CompilerParams(
            collective_id=0, has_side_effects=True, vmem_limit_bytes=56 * 1024 * 1024
        ),
    )(
        spectra.T,
        epoch_weight.reshape(nblocks, BLOCK),
        epoch_unit_local.reshape(nblocks, BLOCK),
        epoch_owner.reshape(nblocks, BLOCK),
        source_blocks,
        coeffs,
        design.T,
    )
    return (new_design.T.astype(F32), new_coeffs)


def solution(mesh):
    return jax.shard_map(
        body,
        mesh=mesh,
        in_specs=(
            P("src", None),
            P(("src", "unit"), None),
            P(("src", "unit")),
            P("src", None),
            P(("src", "unit"), None),
            P(("src", "unit")),
            P("unit", None),
        ),
        out_specs=(P("unit", None), P("src", None)),
        check_vma=False,
    )
```

time: 355 us -> 58.8 us (0.17); the launches traced: 351 us -> 58.6 us
  blocking collectives: 97.4 us -> 0 us
  matrix products: 74.4 us -> 0 us
  local copies, waits for them, and re-layouts: 66.2 us -> 0.6 us
  Pallas kernels: 0 us -> 53.9 us
  other arithmetic: 48.6 us -> 3.46 us
  waiting for transfers between devices: 42.3 us -> 0 us
  between operations: 14.1 us -> 0.65 us
  starting transfers between devices: 6.82 us -> 0 us
    psum x2 -> x0, blocking collectives: 82.5 us -> none  [the longest x1 61.4 us: body(): moment, diag = lax.psum((moment, diag), 'src')]
    dot_general x24 -> x0, matrix products: 74.4 us -> none  [the longest x4 26.5 us: accumulate(): jnp.einsum('bum,bk->umk', spread, coef, preferred_element_type=jnp.float32)]
    pallas_call x0 -> x1, Pallas kernels: none -> 53.9 us  [body(): pl.pallas_call(functools.partial(kernel, n_src, n_unit, nsrc), out_shape=...]
    reshape x12 -> x0, local copies, waits for them, and re-layouts: 36.2 us -> none  [the longest x4 12.6 us: accumulate(): maps = maps.reshape(-1, NSAMP, NCOEF)]
    psum x1 -> x0, waiting for transfers between devices: 32.8 us -> none  [body(): moment, diag = lax.psum((moment, diag), 'src')]
    add x8 -> x0, other arithmetic: 16 us -> none  [the longest x4 14.6 us: accumulate(): return ((carry[0] + moment, carry[1] + diag), None)]
    all_to_all x1 -> x0, blocking collectives: 14.9 us -> none  [body(): lax.all_to_all(per_slot.reshape(parts, cap, 128), 'unit', split_axis=0, c...]
    dot_general x12 -> x0, other arithmetic: 11.3 us -> none  [the longest x4 3.8 us: terms(): jnp.einsum('bmk,bk->bm', local_map, coef, preferred_element_type=jnp.floa...]
  transfers between devices with their start and end apart: 2 -> 0, of which waited for: 2 -> 0; matrix products, arithmetic and copies ran while one was open for 1% -> 0% of each run, Pallas kernels for 0% -> 0%
where the time goes in v3:
time: 58.8 us; the launch traced here: 58.6 us
  Pallas kernels  53.9 us (92%)
  other arithmetic  3.46 us (6%)
  between operations  0.65 us (1%)
  local copies, waits for them, and re-layouts  0.6 us (1%)
    pallas_call x1, Pallas kernels, body(): pl.pallas_call(functools.partial(kernel, n_src, n_unit, nsrc), out_shape=...  53.9 us
    convert_element_type x1, other arithmetic, body(): return (new_design.T.astype(F32), new_coeffs)  3.46 us

profile of v3, /device:TPU:1, one launch (start us, length us, event | category | flops | bytes accessed | tf_op | source)
XLA Modules:
  0.0 58.6 jit_solution(4488347752012866654)
XLA Ops:
  0.6 53.9 %shard_map.86 = (bf16[3300,256]{1,0:T(8,128)(2,1)}, f32[24,55]{1,0:T(8,128)}) custom-call(bf16[60,1024]{1,0:T(8,128)(2,1)} %bitcast.8, bf16[8,128]{1,0:T(8,128)(2,1)} %bitcast.11, s32[8,128]{1,0:T(8,128)} %bitcast.9, s32[8,128]{1,0:T(8,128)} %bitcast.10, s32[1,24]{1,0:T(1,128)} %cnt_hbm.1, f32[24,55]{1,0:T(8,128)} %coef_hbm.1, bf16[3300,256]{1,0:T(8,128)(2,1)} %bitcast.7), custom_call_target="tpu_custom_call" | custom-call | tf_op jit(solution)/shard_map/pallas_call | solution.py:560
  54.5 0.0 copy-start
  54.5 3.5 %convert_bitcast_fusion = f32[256,3300]{0,1:T(8,128)} fusion(bf16[3300,256]{1,0:T(8,128)(2,1)} %get-tuple-element.4), kind=kLoop, calls=%fused_computation | loop fusion | flops 844800 | bytes 5068800 | tf_op jit(solution)/shard_map/convert_element_type | solution.py:628
  58.0 0.0 copy-done
  58.0 0.6 %copy.10 = f32[24,55]{1,0:T(8,128)} copy(f32[24,55]{1,0:T(8,128)S(1)} %copy-done) | data formatting | bytes 10560
Async XLA Ops:
  54.5 3.5 %copy-start = (f32[24,55]{1,0:T(8,128)S(1)}, f32[24,55]{1,0:T(8,128)}, u32[]{:S(2)}) copy-start(f32[24,55]{1,0:T(8,128)} %get-tuple-element.9) | copy-start | bytes 15844

commit v4 on v3

--- a/solution.py
+++ b/solution.py
@@ -82,7 +82,6 @@
     recv2,
     sf_ref,
     w2_ref,
-    wlow_ref,
     emap,
     eflat,
     gbuf,
@@ -115,6 +114,8 @@
     samples = HALF // groups
     part_rows = samples * nsrc
     all_src = n_src * nsrc
+    head = up(nsrc, 16)
+    last_samples = NSAMP - (groups - 1) * samples
     side = math.isqrt(n_src)
     flat = dbuf.shape[0]
     owner_rows = samples * NCOEF
@@ -262,7 +263,6 @@
     dk_ref[...] = maps + dot(pick, dbuf[tail:flat, lanes_half])
 
     unit_row = iota((units, SLOTS), 0).astype(F32)
-    field = iota((HALF, SLOTS), 0)
     source_row = iota((mark_ref.shape[0], SLOTS), 0).astype(F32)
     recv1[0] = out1[0]
 
@@ -279,53 +279,55 @@
         srow = got[62:63]
         table_ref[:, at] = jnp.where(unit_row == urow, wrow, 0.0).astype(BF)
         mark_ref[:, at] = ones_where(jnp.broadcast_to(srow, source_row.shape) == source_row)
-        values = jnp.where(field < NSAMP, got, 0.0)
-        srow = jnp.broadcast_to(srow, (samples, SLOTS))
-        for s in range(0, nsrc, 2):
-            one, two = srow == float(s), srow == float(s + 1)
-            for g in range(groups):
-                data = values[g * samples : (g + 1) * samples]
-                both = jnp.concatenate([jnp.where(one, data, 0.0), jnp.where(two, data, 0.0)], axis=0)
-                base = g * part_rows + s * samples
-                xbuf[base : base + 2 * samples, at] = both.astype(BF)
-
-    high, low = split(dot_nt(mark_ref[...], table_ref[...])[:nsrc])
-    pair = jnp.concatenate([high.astype(F32), low.astype(F32)], axis=0).astype(BF)
-
-    def send2(other):
-        return pltpu.make_async_remote_copy(
-            src_ref=sbuf.at[other],
-            dst_ref=recv2.at[row],
+        chosen = jnp.broadcast_to(srow, (nsrc, SLOTS)) == source_row[:nsrc]
+        for m in range(0, NSAMP, 2):
+            both = [
+                jnp.where(chosen, jnp.broadcast_to(got[n : n + 1], (nsrc, SLOTS)), 0.0)
+                for n in (m, m + 1)
+            ]
+            xbuf[m * nsrc : (m + 2) * nsrc, at] = jnp.concatenate(both, axis=0).astype(BF)
+
+    weight_own = dot_nt(mark_ref[...], table_ref[...]).astype(BF)
+
+    def copy2(other, slot, rows):
+        return pltpu.make_async_remote_copy(
+            src_ref=sbuf.at[other, pl.ds(0, rows)],
+            dst_ref=recv2.at[slot, pl.ds(0, rows)],
             send_sem=ssem2.at[other],
-            recv_sem=rsem2.at[row],
+            recv_sem=rsem2.at[slot],
             device_id={"src": other},
             device_id_type=MESH,
         )
 
-    def came2(other):
-        return pltpu.make_async_remote_copy(
-            src_ref=sbuf.at[other],
-            dst_ref=recv2.at[other],
-            send_sem=ssem2.at[other],
-            recv_sem=rsem2.at[other],
-            device_id={"src": other},
-            device_id_type=MESH,
-        )
+    def by_group(group, act):
+        @pl.when(group < groups - 1)
+        def _():
+            act(head + part_rows)
+
+        @pl.when(group == groups - 1)
+        def _():
+            act(head + last_samples * nsrc)
 
     @loop(0, groups)
     def _(k):
-        group = lax.rem(my_group + 1 + k, groups)
+        if side == 4:
+            turn = lax.rem(k, 4)
+            dy = jnp.where(turn == 0, 2, jnp.where(turn == 1, 1, jnp.where(turn == 2, 3, 0)))
+            dx = jnp.where(k < 4, jnp.where(k == 1, 0, 1), jnp.where(k == 5, 1, 0))
+            group = lax.rem(my_group // side + dx, 2) * side + lax.rem(my_group + dy, side)
+        else:
+            group = lax.rem(my_group + 1 + k, groups)
         x = xbuf[pl.ds(pl.multiple_of(group * part_rows, part_rows), part_rows), :]
         sums = dot_nt(x, table_ref[...]).astype(BF)
         for half in range(2):
             other = half * groups + group
             lanes = slice(half * LANES, (half + 1) * LANES)
-            sbuf[other, 0:part_rows, :] = sums[:, lanes]
-            sbuf[other, part_rows : part_rows + 2 * nsrc, :] = pair[:, lanes]
+            sbuf[other, 0:head, :] = weight_own[:, lanes]
+            sbuf[other, head : head + part_rows, :] = sums[:, lanes]
 
             @pl.when(other != row)
             def _():
-                send2(other).start()
+                by_group(group, lambda rows: copy2(other, row, rows).start())
 
     recv2[row] = sbuf[row]
 
@@ -346,31 +348,41 @@
 
         @pl.when(i > 0)
         def _():
-            came2(r).wait_recv()
+            by_group(my_group, lambda rows: copy2(r, r, rows).wait_recv())
 
         got = recv2[r].astype(F32)
-        sf_ref[pl.ds(pl.multiple_of(r * part_rows, part_rows), part_rows), :] = got[:part_rows]
-        at = pl.ds(pl.multiple_of(r * nsrc, 8), nsrc)
-        w2_ref[at, :] = got[part_rows : part_rows + nsrc] + got[part_rows + nsrc :]
+        for m in range(samples):
+            at = pl.ds(pl.multiple_of(m * all_src + r * nsrc, 8), nsrc)
+            sf_ref[at, :] = got[head + m * nsrc : head + (m + 1) * nsrc]
+        w2_ref[pl.ds(pl.multiple_of(r * nsrc, 8), nsrc), :] = got[:nsrc]
 
     coef = c_ref[...]
     turned = coef.T[:HALF]
     turned_lo = turned.astype(BF)
     square_hi, square_lo = split(turned * turned)
     coef_all = coef[:, :HALF].astype(BF)
-    weight_hi, weight_lo = split(w2_ref[...])
-    wlow_ref[0] = weight_hi
-    wlow_ref[1] = weight_lo
-    diag = dot(square_hi, weight_hi) + dot(square_lo, weight_hi) + dot(square_hi, weight_lo)
+    weight_lo = w2_ref[...].astype(BF)
+    diag = dot(square_hi, weight_lo) + dot(square_lo, weight_lo)
     scale = 1.0 / (diag + damping)
 
-    for m in range(samples):
+    def by_samples(act):
+        for m in range(last_samples):
+            act(m)
+
+        @pl.when(my_group < groups - 1)
+        def _():
+            for m in range(last_samples, samples):
+                act(m)
+
+    def refine(m):
         base = dk_ref[m * HALF : (m + 1) * HALF, :]
-        sums = sf_ref[pl.ds(m, all_src, stride=samples), :]
+        sums = sf_ref[m * all_src : (m + 1) * all_src, :]
         resid = (sums - w2_ref[...] * dot(coef_all, base.astype(BF))).astype(BF)
         refined = (base + dot(turned_lo, resid) * scale).astype(BF).astype(F32)
         emap[m] = refined
         dk_ref[m * NCOEF : (m + 1) * NCOEF, :] = refined[:NCOEF]
+
+    by_samples(refine)
     if owner_rows < eflat.shape[0]:
         dk_ref[owner_rows : eflat.shape[0], :] = jnp.zeros((eflat.shape[0] - owner_rows, LANES), F32)
     eflat[...] = dk_ref[0 : eflat.shape[0], :].astype(BF)
@@ -416,31 +428,44 @@
             device_id_type=MESH,
         )
 
+    def whole(half, origin):
+        if half == 0 or last_samples * NCOEF > half_rows:
+            return origin >= 0
+        return origin % groups != groups - 1
+
     gbuf[row] = eflat[...]
 
     @loop(1, side)
     def _(d):
         for half in range(2):
-            stage1(half, d).start()
+
+            @pl.when(whole(half, row))
+            def _():
+                stage1(half, d).start()
 
     @loop(1, side)
     def _(d):
         for half in range(2):
-            stage2(half, 0, d).start()
+
+            @pl.when(whole(half, row))
+            def _():
+                stage2(half, 0, d).start()
 
     gh_ref[...] = jnp.zeros_like(gh_ref)
     csq_ref[...] = jnp.zeros_like(csq_ref)
     blank = jnp.zeros((HALF, LANES), F32)
-    for m in range(samples):
+
+    def terms(m):
         refined = emap[m]
-        sums = sf_ref[pl.ds(m, all_src, stride=samples), :]
+        sums = sf_ref[m * all_src : (m + 1) * all_src, :]
         resid = (sums - w2_ref[...] * dot(coef_all, refined.astype(BF))).astype(BF)
         gh_ref[...] += dot_nt(resid, jnp.concatenate([refined, blank], axis=0).astype(BF))
         csq_ref[...] += refined * refined
+
+    by_samples(terms)
     curve_hi, curve_lo = split(jnp.concatenate([blank, csq_ref[...]], axis=0))
-    gh_ref[...] += (
-        dot_nt(wlow_ref[0], curve_hi) + dot_nt(wlow_ref[0], curve_lo) + dot_nt(wlow_ref[1], curve_hi)
-    )
+    weight_lo = w2_ref[...].astype(BF)
+    gh_ref[...] += dot_nt(weight_lo, curve_hi) + dot_nt(weight_lo, curve_lo)
 
     def send3(i):
         return pltpu.make_async_remote_copy(
@@ -459,11 +484,14 @@
     @loop(1, side)
     def _(q):
         for half in range(2):
-            came5(half, peer(half, q)).wait_recv()
-
-            @loop(1, side)
-            def _(d):
-                stage2(half, q, d).start()
+
+            @pl.when(whole(half, peer(half, q)))
+            def _():
+                came5(half, peer(half, q)).wait_recv()
+
+                @loop(1, side)
+                def _(d):
+                    stage2(half, q, d).start()
 
     g1_ref[...] = gh_ref[pl.ds(pl.multiple_of(row * nsrc, 8), nsrc), :]
 
@@ -502,7 +530,7 @@
         for half in range(2):
             same = (other // side == px) if half == 1 else (other % side == py)
 
-            @pl.when(jnp.logical_not(same))
+            @pl.when(jnp.logical_not(same) & whole(half, other))
             def _():
                 came5(half, other).wait_recv()
 
@@ -529,15 +557,23 @@
     @loop(1, n_src)
     def _(i):
         send_coef(i).wait_send()
-        send2(row_at(i)).wait_send()
         send3(i).wait_send()
+        other = row_at(i)
+        by_group(other % groups, lambda rows: copy2(other, row, rows).wait_send())
 
     @loop(1, side)
     def _(d):
         for half in range(2):
-            stage1(half, d).wait_send()
+
+            @pl.when(whole(half, row))
+            def _():
+                stage1(half, d).wait_send()
+
             for q in range(side):
-                stage2(half, q, d).wait_send()
+
+                @pl.when(whole(half, peer(half, q)))
+                def _():
+                    stage2(half, q, d).wait_send()
 
 
 def body(coeffs, spectra, epoch_weight, source_blocks, epoch_owner, epoch_unit_local, design):
@@ -550,7 +586,7 @@
     groups = n_src // 2
     samples = HALF // groups
     part_rows = samples * nsrc
-    message = part_rows + 2 * nsrc
+    message = part_rows + up(nsrc, 16)
     all_src = n_src * nsrc
     side = math.isqrt(n_src)
     erows = up(samples * NCOEF, 32)
@@ -589,7 +625,6 @@
             pltpu.VMEM((n_src, message, LANES), BF),
             pltpu.VMEM((n_src * part_rows, LANES), F32),
             pltpu.VMEM((all_src, LANES), F32),
-            pltpu.VMEM((2, all_src, LANES), BF),
             pltpu.VMEM((samples, HALF, LANES), F32),
             pltpu.VMEM((erows, LANES), BF),
             pltpu.VMEM((n_src, erows, LANES), BF),
@@ -614,16 +649,21 @@
             sems((2, n_src)),
         ],
         compiler_params=pltpu.CompilerParams(
-            collective_id=0, has_side_effects=True, vmem_limit_bytes=56 * 1024 * 1024
+            collective_id=0, has_side_effects=True, vmem_limit_bytes=44 * 1024 * 1024
         ),
     )(
-        spectra.T,
-        epoch_weight.reshape(nblocks, BLOCK),
-        epoch_unit_local.reshape(nblocks, BLOCK),
-        epoch_owner.reshape(nblocks, BLOCK),
-        source_blocks,
-        coeffs,
-        design.T,
+        *[
+            pltpu.with_memory_space_constraint(x, pltpu.HBM)
+            for x in (
+                spectra.T,
+                epoch_weight.reshape(nblocks, BLOCK),
+                epoch_unit_local.reshape(nblocks, BLOCK),
+                epoch_owner.reshape(nblocks, BLOCK),
+                source_blocks,
+                coeffs,
+                design.T,
+            )
+        ]
     )
     return (new_design.T.astype(F32), new_coeffs)
 

time: 58.8 us -> 53.5 us (0.910)
  Pallas kernels: 53.9 us -> 50.2 us
  other arithmetic: 3.46 us -> 2.01 us
    pallas_call x1, Pallas kernels: 53.9 us -> 50.2 us  [body(): pl.pallas_call(functools.partial(kernel, n_src, n_unit, nsrc), out_shape=...]
    convert_element_type x1, other arithmetic: 3.46 us -> 2.01 us  [body(): return (new_design.T.astype(F32), new_coeffs)]
where the time goes in v4:
time: 53.5 us; the launch traced here: 53.4 us
  Pallas kernels  50.2 us (94%)
  other arithmetic  2.01 us (4%)
  between operations  0.64 us (1%)
  local copies, waits for them, and re-layouts  0.6 us (1%)
    pallas_call x1, Pallas kernels, body(): pl.pallas_call(functools.partial(kernel, n_src, n_unit, nsrc), out_shape=...  50.2 us
    convert_element_type x1, other arithmetic, body(): return (new_design.T.astype(F32), new_coeffs)  2.01 us

profile of v4, /device:TPU:1, one launch (start us, length us, event | category | flops | bytes accessed | tf_op | source)
XLA Modules:
  0.0 53.4 jit_solution(8029499329567579181)
XLA Ops:
  0.6 50.2 %shard_map.86 = (bf16[3300,256]{1,0:T(8,128)(2,1)S(1)}, f32[24,55]{1,0:T(8,128)S(1)}) custom-call(bf16[60,1024]{1,0:T(8,128)(2,1)} %bitcast.8, bf16[8,128]{1,0:T(8,128)(2,1)} %bitcast.11, s32[8,128]{1,0:T(8,128)} %bitcast.9, s32[8,128]{1,0:T(8,128)} %bitcast.10, s32[1,24]{1,0:T(1,128)} %cnt_hbm.1, f32[24,55]{1,0:T(8,128)} %coef_hbm.1, bf16[3300,256]{1,0:T(8,128)(2,1)} %bitcast.7), custom_call_target="tpu_custom_call" | custom-call | tf_op jit(solution)/shard_map/pallas_call | solution.py:596
  50.8 2.0 %convert_bitcast_fusion = f32[256,3300]{0,1:T(8,128)} fusion(bf16[3300,256]{1,0:T(8,128)(2,1)S(1)} %get-tuple-element.4), kind=kLoop, calls=%fused_computation | loop fusion | flops 844800 | bytes 5068800 | tf_op jit(solution)/shard_map/convert_element_type | solution.py:668
  52.8 0.6 %copy.10 = f32[24,55]{1,0:T(8,128)} copy(f32[24,55]{1,0:T(8,128)S(1)} %get-tuple-element.9) | data formatting | bytes 10560

commit v5 on v4

--- a/solution.py
+++ b/solution.py
@@ -77,6 +77,7 @@
     dk_ref,
     table_ref,
     mark_ref,
+    got_ref,
     xbuf,
     sbuf,
     recv2,
@@ -102,7 +103,6 @@
     ssem4,
     rsem4,
     ssem5,
-    ssem6,
     rsem5,
 ):
     row = lax.axis_index("src")
@@ -224,15 +224,16 @@
             device_id_type=MESH,
         )
 
-    slot = iota((SLOTS, LANES), 0).astype(F32)
+    slot = iota((SLOTS, LANES), 0).astype(F32).astype(BF)
+    one, zero = jnp.ones((), BF), jnp.zeros((), BF)
 
     @loop(0, n_unit)
     def _(k):
         i = lax.rem(k + 1, n_unit)
         ranks = rank_ref[pl.ds(pl.multiple_of(unit_at(i) * nblocks, nblocks), nblocks), :]
         for block in range(nblocks):
-            line = jnp.broadcast_to(ranks[block : block + 1, :], (SLOTS, LANES))
-            place_ref[:, block * BLOCK : (block + 1) * BLOCK] = ones_where(line == slot)
+            line = jnp.broadcast_to(ranks[block : block + 1, :], (SLOTS, LANES)).astype(BF)
+            place_ref[:, block * BLOCK : (block + 1) * BLOCK] = jnp.where(line == slot, one, zero)
         result = dot_nt(items_ref[...], place_ref[...]).astype(BF)
         out1[i] = result
 
@@ -277,17 +278,12 @@
         wrow = jnp.broadcast_to(got[60:61], (units, SLOTS))
         urow = jnp.broadcast_to(got[61:62], (units, SLOTS))
         srow = got[62:63]
-        table_ref[:, at] = jnp.where(unit_row == urow, wrow, 0.0).astype(BF)
-        mark_ref[:, at] = ones_where(jnp.broadcast_to(srow, source_row.shape) == source_row)
-        chosen = jnp.broadcast_to(srow, (nsrc, SLOTS)) == source_row[:nsrc]
-        for m in range(0, NSAMP, 2):
-            both = [
-                jnp.where(chosen, jnp.broadcast_to(got[n : n + 1], (nsrc, SLOTS)), 0.0)
-                for n in (m, m + 1)
-            ]
-            xbuf[m * nsrc : (m + 2) * nsrc, at] = jnp.concatenate(both, axis=0).astype(BF)
-
-    weight_own = dot_nt(mark_ref[...], table_ref[...]).astype(BF)
+        table_ref[at, :] = jnp.where(unit_row == urow, wrow, 0.0).T.astype(BF)
+        chosen = jnp.broadcast_to(srow, source_row.shape) == source_row
+        mark_ref[:, at] = jnp.where(chosen, 1.0, 0.0)
+        got_ref[:, at] = got
+
+    weight_own = dot(mark_ref[...].astype(BF), table_ref[...]).astype(BF)
 
     def copy2(other, slot, rows):
         return pltpu.make_async_remote_copy(
@@ -317,8 +313,12 @@
             group = lax.rem(my_group // side + dx, 2) * side + lax.rem(my_group + dy, side)
         else:
             group = lax.rem(my_group + 1 + k, groups)
-        x = xbuf[pl.ds(pl.multiple_of(group * part_rows, part_rows), part_rows), :]
-        sums = dot_nt(x, table_ref[...]).astype(BF)
+        data = got_ref[pl.ds(pl.multiple_of(group * samples, 8), samples), :]
+        chosen = mark_ref[0:nsrc, :]
+        for m in range(0, samples, 2):
+            both = [chosen * data[n : n + 1] for n in (m, m + 1)]
+            xbuf[m * nsrc : (m + 2) * nsrc, :] = jnp.concatenate(both, axis=0).astype(BF)
+        sums = dot(xbuf[...], table_ref[...]).astype(BF)
         for half in range(2):
             other = half * groups + group
             lanes = slice(half * LANES, (half + 1) * LANES)
@@ -388,43 +388,23 @@
     eflat[...] = dk_ref[0 : eflat.shape[0], :].astype(BF)
 
     px, py = row // side, row % side
-
-    def peer(axis, d):
-        if axis == 0:
-            return lax.rem(px + d, side) * side + py
-        return px * side + lax.rem(py + d, side)
-
-    def piece(half):
-        return pl.ds(half * half_rows, half_rows)
-
-    def stage1(half, d):
+    part_piece = half_rows // 2
+
+    def at_offset(half, first, second):
+        dx, dy = (first, second) if half == 0 else (second, first)
+        return lax.rem(px + dx, side) * side + lax.rem(py + dy, side)
+
+    def pass_on(half, origin, sub, target, key):
+        if sub is None:
+            rows = pl.ds(half * half_rows, half_rows)
+        else:
+            rows = pl.ds(half * half_rows + sub * part_piece, part_piece)
         return pltpu.make_async_remote_copy(
-            src_ref=eflat.at[piece(half)],
-            dst_ref=gbuf.at[row, piece(half)],
-            send_sem=ssem5.at[half, d],
-            recv_sem=rsem5.at[half, row],
-            device_id={"src": peer(half, d)},
-            device_id_type=MESH,
-        )
-
-    def stage2(half, q, d):
-        origin = peer(half, q)
-        return pltpu.make_async_remote_copy(
-            src_ref=gbuf.at[origin, piece(half)],
-            dst_ref=gbuf.at[origin, piece(half)],
-            send_sem=ssem6.at[half, q, d],
-            recv_sem=rsem5.at[half, origin],
-            device_id={"src": peer(1 - half, d)},
-            device_id_type=MESH,
-        )
-
-    def came5(half, origin):
-        return pltpu.make_async_remote_copy(
-            src_ref=gbuf.at[origin, piece(half)],
-            dst_ref=gbuf.at[origin, piece(half)],
-            send_sem=ssem5.at[half, 0],
-            recv_sem=rsem5.at[half, origin],
-            device_id={"src": row_at(1)},
+            src_ref=gbuf.at[origin, rows],
+            dst_ref=gbuf.at[origin, rows],
+            send_sem=ssem5.at[half, key[0], key[1]],
+            recv_sem=rsem5.at[half, origin, sub or 0],
+            device_id={"src": target},
             device_id_type=MESH,
         )
 
@@ -433,23 +413,34 @@
             return origin >= 0
         return origin % groups != groups - 1
 
+    back, two = side - 1, side // 2
+    ways = (1, back)
+    relayed = (0, 1, back)
+
+    def send_block(half, q):
+        for n, way in enumerate(ways if q in relayed else (1, two, back)):
+            pass_on(half, at_offset(half, q, 0), None, at_offset(half, 0, way), (q, n)).start()
+
+    def arrived(half, origin, sub):
+        pass_on(half, origin, sub, at_offset(half, 1, 0), (0, 0)).wait_recv()
+
+    def relay(half, q):
+        for n, way in enumerate(ways):
+            origin = at_offset(half, q, (back, 1)[n])
+
+            @pl.when(whole(half, origin))
+            def _():
+                arrived(half, origin, None)
+                pass_on(half, origin, n, at_offset(half, 0, way), (q, 3 + n)).start()
+
     gbuf[row] = eflat[...]
-
-    @loop(1, side)
-    def _(d):
-        for half in range(2):
-
-            @pl.when(whole(half, row))
-            def _():
-                stage1(half, d).start()
-
-    @loop(1, side)
-    def _(d):
-        for half in range(2):
-
-            @pl.when(whole(half, row))
-            def _():
-                stage2(half, 0, d).start()
+    for half in range(2):
+
+        @pl.when(whole(half, row))
+        def _():
+            for n, way in enumerate((two, 1, back)):
+                pass_on(half, row, None, at_offset(half, way, 0), (side, n)).start()
+            send_block(half, 0)
 
     gh_ref[...] = jnp.zeros_like(gh_ref)
     csq_ref[...] = jnp.zeros_like(csq_ref)
@@ -481,18 +472,23 @@
     def _(i):
         send3(i).start()
 
-    @loop(1, side)
-    def _(q):
+    def forward(q):
         for half in range(2):
-
-            @pl.when(whole(half, peer(half, q)))
+            origin = at_offset(half, q, 0)
+
+            @pl.when(whole(half, origin))
             def _():
-                came5(half, peer(half, q)).wait_recv()
-
-                @loop(1, side)
-                def _(d):
-                    stage2(half, q, d).start()
-
+                arrived(half, origin, None)
+                send_block(half, q)
+
+    def ring(q):
+        for half in range(2):
+            relay(half, q)
+
+    forward(1)
+    forward(back)
+    ring(0)
+    forward(two)
     g1_ref[...] = gh_ref[pl.ds(pl.multiple_of(row * nsrc, 8), nsrc), :]
 
     @loop(1, n_src)
@@ -514,6 +510,30 @@
     def _(i):
         send4(i).start()
 
+    ring(1)
+    ring(back)
+
+    for q in range(side):
+        for half in range(2):
+            for way in (two,) if q in relayed else (1, back, two):
+                origin = at_offset(half, q, way)
+
+                @pl.when(whole(half, origin))
+                def _():
+                    for sub in (0, 1) if q in relayed else (None,):
+                        arrived(half, origin, sub)
+
+    for half in range(2):
+        lanes = slice(half * LANES, (half + 1) * LANES)
+
+        @loop(0, groups - 1)
+        def _(group):
+            at = pl.ds(pl.multiple_of(group * owner_rows, 8), owner_rows)
+            out_ref[at, lanes] = gbuf[half * groups + group][:owner_rows]
+
+        done_rows = (groups - 1) * owner_rows
+        out_ref[done_rows:flat, lanes] = gbuf[half * groups + groups - 1][: flat - done_rows]
+
     recv4[me] = g1_ref[...]
 
     @loop(1, n_unit)
@@ -526,29 +546,6 @@
     step = total / (pltpu.roll(total, HALF, 1) + damping)
     nc_ref[...] = coef_ref[...] + step[:, :NCOEF]
 
-    def arrive(other):
-        for half in range(2):
-            same = (other // side == px) if half == 1 else (other % side == py)
-
-            @pl.when(jnp.logical_not(same) & whole(half, other))
-            def _():
-                came5(half, other).wait_recv()
-
-    for half in range(2):
-        lanes = slice(half * LANES, (half + 1) * LANES)
-
-        @loop(0, groups - 1)
-        def _(group):
-            other = half * groups + group
-            arrive(other)
-            at = pl.ds(pl.multiple_of(group * owner_rows, 8), owner_rows)
-            out_ref[at, lanes] = gbuf[other][:owner_rows]
-
-        other = half * groups + groups - 1
-        arrive(other)
-        done_rows = (groups - 1) * owner_rows
-        out_ref[done_rows:flat, lanes] = gbuf[other][: flat - done_rows]
-
     @loop(1, n_unit)
     def _(i):
         send1(i).wait_send()
@@ -561,19 +558,25 @@
         other = row_at(i)
         by_group(other % groups, lambda rows: copy2(other, row, rows).wait_send())
 
-    @loop(1, side)
-    def _(d):
-        for half in range(2):
-
-            @pl.when(whole(half, row))
+    for half in range(2):
+        for q in range(side):
+
+            @pl.when(whole(half, at_offset(half, q, 0)))
             def _():
-                stage1(half, d).wait_send()
-
-            for q in range(side):
-
-                @pl.when(whole(half, peer(half, q)))
-                def _():
-                    stage2(half, q, d).wait_send()
+                for n in range(2 if q in relayed else 3):
+                    pass_on(half, row, None, at_offset(half, 1, 0), (q, n)).wait_send()
+
+            if q in relayed:
+                for n in range(2):
+
+                    @pl.when(whole(half, at_offset(half, q, (back, 1)[n])))
+                    def _():
+                        pass_on(half, row, n, at_offset(half, 1, 0), (q, 3 + n)).wait_send()
+
+        @pl.when(whole(half, row))
+        def _():
+            for n in range(3):
+                pass_on(half, row, None, at_offset(half, 1, 0), (side, n)).wait_send()
 
 
 def body(coeffs, spectra, epoch_weight, source_blocks, epoch_owner, epoch_unit_local, design):
@@ -589,7 +592,7 @@
     message = part_rows + up(nsrc, 16)
     all_src = n_src * nsrc
     side = math.isqrt(n_src)
-    erows = up(samples * NCOEF, 32)
+    erows = up(samples * NCOEF, 64)
     vmem = pl.BlockSpec(memory_space=pltpu.VMEM)
     hbm = pl.BlockSpec(memory_space=pltpu.HBM)
     sems = pltpu.SemaphoreType.DMA
@@ -618,9 +621,10 @@
             pltpu.VMEM((n_src, up(nsrc, 16), LANES), BF),
             pltpu.VMEM((all_src, LANES), F32),
             pltpu.VMEM((samples * HALF, LANES), F32),
-            pltpu.VMEM((units, n_unit * SLOTS), BF),
-            pltpu.VMEM((up(nsrc, 16), n_unit * SLOTS), BF),
-            pltpu.VMEM((groups * part_rows, n_unit * SLOTS), BF),
+            pltpu.VMEM((n_unit * SLOTS, units), BF),
+            pltpu.VMEM((up(nsrc, 16), n_unit * SLOTS), F32),
+            pltpu.VMEM((HALF, n_unit * SLOTS), F32),
+            pltpu.VMEM((part_rows, n_unit * SLOTS), BF),
             pltpu.VMEM((n_src, message, LANES), BF),
             pltpu.VMEM((n_src, message, LANES), BF),
             pltpu.VMEM((n_src * part_rows, LANES), F32),
@@ -644,9 +648,8 @@
             sems((n_src,)),
             sems((n_unit,)),
             sems((n_unit,)),
-            sems((2, side)),
-            sems((2, side, side)),
-            sems((2, n_src)),
+            sems((2, side + 1, 5)),
+            sems((2, n_src, 2)),
         ],
         compiler_params=pltpu.CompilerParams(
             collective_id=0, has_side_effects=True, vmem_limit_bytes=44 * 1024 * 1024

time: 53.5 us -> 51.3 us (0.959); the launches traced: 53.4 us -> 50.6 us
  Pallas kernels: 50.2 us -> 47.3 us
    pallas_call x1, Pallas kernels: 50.2 us -> 47.3 us  [body(): pl.pallas_call(functools.partial(kernel, n_src, n_unit, nsrc), out_shape=...]
where the time goes in v5:
time: 51.3 us; the launch traced here: 50.6 us
  Pallas kernels  47.3 us (92%)
  other arithmetic  2.01 us (4%)
  between operations  0.64 us (1%)
  local copies, waits for them, and re-layouts  0.6 us (1%)
    pallas_call x1, Pallas kernels, body(): pl.pallas_call(functools.partial(kernel, n_src, n_unit, nsrc), out_shape=...  47.3 us
    convert_element_type x1, other arithmetic, body(): return (new_design.T.astype(F32), new_coeffs)  2.01 us

profile of v5, /device:TPU:1, one launch (start us, length us, event | category | flops | bytes accessed | tf_op | source)
XLA Modules:
  0.0 50.6 jit_solution(5889924788518061423)
XLA Ops:
  0.6 47.3 %shard_map.86 = (bf16[3300,256]{1,0:T(8,128)(2,1)S(1)}, f32[24,55]{1,0:T(8,128)S(1)}) custom-call(bf16[60,1024]{1,0:T(8,128)(2,1)} %bitcast.8, bf16[8,128]{1,0:T(8,128)(2,1)} %bitcast.11, s32[8,128]{1,0:T(8,128)} %bitcast.9, s32[8,128]{1,0:T(8,128)} %bitcast.10, s32[1,24]{1,0:T(1,128)} %cnt_hbm.1, f32[24,55]{1,0:T(8,128)} %coef_hbm.1, bf16[3300,256]{1,0:T(8,128)(2,1)} %bitcast.7), custom_call_target="tpu_custom_call" | custom-call | tf_op jit(solution)/shard_map/pallas_call | solution.py:599
  48.0 2.0 %convert_bitcast_fusion = f32[256,3300]{0,1:T(8,128)} fusion(bf16[3300,256]{1,0:T(8,128)(2,1)S(1)} %get-tuple-element.4), kind=kLoop, calls=%fused_computation | loop fusion | flops 844800 | bytes 5068800 | tf_op jit(solution)/shard_map/convert_element_type | solution.py:671
  50.0 0.6 %copy.10 = f32[24,55]{1,0:T(8,128)} copy(f32[24,55]{1,0:T(8,128)S(1)} %get-tuple-element.9) | data formatting | bytes 10560

commit v6 on v5

--- a/solution.py
+++ b/solution.py
@@ -57,7 +57,7 @@
     cnt_hbm,
     coef_hbm,
     design_hbm,
-    out_ref,
+    gbuf,
     nc_ref,
     spec_ref,
     w_ref,
@@ -82,10 +82,10 @@
     sbuf,
     recv2,
     sf_ref,
+    ahead_ref,
     w2_ref,
     emap,
     eflat,
-    gbuf,
     gh_ref,
     csq_ref,
     recv3,
@@ -224,12 +224,16 @@
             device_id_type=MESH,
         )
 
+    def far_first(k):
+        middle = n_unit // 2
+        return lax.rem(middle + jnp.where(k % 2 == 1, (k + 1) // 2, n_unit - k // 2), n_unit)
+
     slot = iota((SLOTS, LANES), 0).astype(F32).astype(BF)
     one, zero = jnp.ones((), BF), jnp.zeros((), BF)
 
     @loop(0, n_unit)
     def _(k):
-        i = lax.rem(k + 1, n_unit)
+        i = far_first(k)
         ranks = rank_ref[pl.ds(pl.multiple_of(unit_at(i) * nblocks, nblocks), nblocks), :]
         for block in range(nblocks):
             line = jnp.broadcast_to(ranks[block : block + 1, :], (SLOTS, LANES)).astype(BF)
@@ -268,7 +272,9 @@
     recv1[0] = out1[0]
 
     @loop(0, n_unit)
-    def _(i):
+    def _(k):
+        i = jnp.where(k == 0, 0, far_first(k - 1))
+
         @pl.when(i > 0)
         def _():
             send1(i).wait_recv()
@@ -342,6 +348,14 @@
         at = pl.ds(pl.multiple_of(r * nsrc, 8), nsrc)
         c_ref[at, :] = crecv[r].astype(F32)[:nsrc]
 
+    coef = c_ref[...]
+    turned = coef.T[:HALF]
+    turned_lo = turned.astype(BF)
+    square_hi, square_lo = split(turned * turned)
+    coef_all = coef[:, :HALF].astype(BF)
+    for m in range(samples):
+        ahead_ref[m] = dot(coef_all, dk_ref[m * HALF : (m + 1) * HALF, :].astype(BF))
+
     @loop(0, n_src)
     def _(i):
         r = row_at(i)
@@ -356,11 +370,6 @@
             sf_ref[at, :] = got[head + m * nsrc : head + (m + 1) * nsrc]
         w2_ref[pl.ds(pl.multiple_of(r * nsrc, 8), nsrc), :] = got[:nsrc]
 
-    coef = c_ref[...]
-    turned = coef.T[:HALF]
-    turned_lo = turned.astype(BF)
-    square_hi, square_lo = split(turned * turned)
-    coef_all = coef[:, :HALF].astype(BF)
     weight_lo = w2_ref[...].astype(BF)
     diag = dot(square_hi, weight_lo) + dot(square_lo, weight_lo)
     scale = 1.0 / (diag + damping)
@@ -377,7 +386,7 @@
     def refine(m):
         base = dk_ref[m * HALF : (m + 1) * HALF, :]
         sums = sf_ref[m * all_src : (m + 1) * all_src, :]
-        resid = (sums - w2_ref[...] * dot(coef_all, base.astype(BF))).astype(BF)
+        resid = (sums - w2_ref[...] * ahead_ref[m]).astype(BF)
         refined = (base + dot(turned_lo, resid) * scale).astype(BF).astype(F32)
         emap[m] = refined
         dk_ref[m * NCOEF : (m + 1) * NCOEF, :] = refined[:NCOEF]
@@ -523,17 +532,6 @@
                     for sub in (0, 1) if q in relayed else (None,):
                         arrived(half, origin, sub)
 
-    for half in range(2):
-        lanes = slice(half * LANES, (half + 1) * LANES)
-
-        @loop(0, groups - 1)
-        def _(group):
-            at = pl.ds(pl.multiple_of(group * owner_rows, 8), owner_rows)
-            out_ref[at, lanes] = gbuf[half * groups + group][:owner_rows]
-
-        done_rows = (groups - 1) * owner_rows
-        out_ref[done_rows:flat, lanes] = gbuf[half * groups + groups - 1][: flat - done_rows]
-
     recv4[me] = g1_ref[...]
 
     @loop(1, n_unit)
@@ -577,6 +575,42 @@
         def _():
             for n in range(3):
                 pass_on(half, row, None, at_offset(half, 1, 0), (side, n)).wait_send()
+
+
+def widen_kernel(step, in_ref, nc_in, out_hbm, nc_hbm, wide_ref, sems):
+    groups = in_ref.shape[0] // 2
+    flat = wide_ref.shape[0]
+    copies = [pltpu.make_async_copy(nc_in, nc_hbm, sems.at[groups])]
+    copies[0].start()
+    for group in range(groups):
+        first, last = group * step, min((group + 1) * step, flat)
+        for half in range(2):
+            lanes = slice(half * LANES, (half + 1) * LANES)
+            wide_ref[first:last, lanes] = in_ref[half * groups + group].astype(F32)[: last - first]
+        rows = pl.ds(first, last - first)
+        copies.append(pltpu.make_async_copy(wide_ref.at[rows], out_hbm.at[rows], sems.at[group]))
+        copies[-1].start()
+    for copy in copies:
+        copy.wait()
+
+
+def widen(gathered, new_coeffs, flat, step):
+    vmem = pl.BlockSpec(memory_space=pltpu.VMEM)
+    hbm = pl.BlockSpec(memory_space=pltpu.HBM)
+    return pl.pallas_call(
+        functools.partial(widen_kernel, step),
+        out_shape=(
+            jax.ShapeDtypeStruct((flat, 2 * LANES), F32),
+            jax.ShapeDtypeStruct(new_coeffs.shape, F32),
+        ),
+        in_specs=[vmem, vmem],
+        out_specs=(hbm, hbm),
+        scratch_shapes=[
+            pltpu.VMEM((flat, 2 * LANES), F32),
+            pltpu.SemaphoreType.DMA((gathered.shape[0] // 2 + 1,)),
+        ],
+        compiler_params=pltpu.CompilerParams(vmem_limit_bytes=16 * 1024 * 1024),
+    )(gathered, new_coeffs)
 
 
 def body(coeffs, spectra, epoch_weight, source_blocks, epoch_owner, epoch_unit_local, design):
@@ -596,10 +630,10 @@
     vmem = pl.BlockSpec(memory_space=pltpu.VMEM)
     hbm = pl.BlockSpec(memory_space=pltpu.HBM)
     sems = pltpu.SemaphoreType.DMA
-    new_design, new_coeffs = pl.pallas_call(
+    gathered, new_coeffs = pl.pallas_call(
         functools.partial(kernel, n_src, n_unit, nsrc),
         out_shape=(
-            jax.ShapeDtypeStruct((flat, units), BF),
+            jax.ShapeDtypeStruct((n_src, erows, LANES), BF),
             jax.ShapeDtypeStruct(coeffs.shape, F32),
         ),
         in_specs=[hbm] * 7,
@@ -628,10 +662,10 @@
             pltpu.VMEM((n_src, message, LANES), BF),
             pltpu.VMEM((n_src, message, LANES), BF),
             pltpu.VMEM((n_src * part_rows, LANES), F32),
+            pltpu.VMEM((samples, all_src, LANES), F32),
             pltpu.VMEM((all_src, LANES), F32),
             pltpu.VMEM((samples, HALF, LANES), F32),
             pltpu.VMEM((erows, LANES), BF),
-            pltpu.VMEM((n_src, erows, LANES), BF),
             pltpu.VMEM((all_src, LANES), F32),
             pltpu.VMEM((HALF, LANES), F32),
             pltpu.VMEM((n_src, nsrc, LANES), F32),
@@ -668,7 +702,8 @@
             )
         ]
     )
-    return (new_design.T.astype(F32), new_coeffs)
+    new_design, new_coeffs = widen(gathered, new_coeffs, flat, samples * NCOEF)
+    return (new_design.T, new_coeffs)
 
 
 def solution(mesh):

time: 51.3 us -> 48.4 us (0.943)
  other arithmetic: 2.01 us -> 0 us
  local copies, waits for them, and re-layouts: 0.6 us -> 0 us
    convert_element_type x1 -> x0, other arithmetic: 2.01 us -> none  [body(): return (new_design.T.astype(F32), new_coeffs)]
    pallas_call x0 -> x1, Pallas kernels: none -> 1.84 us  [widen(): pl.pallas_call(functools.partial(widen_kernel, step), out_shape=(jax.Shap...]
    pallas_call x1, Pallas kernels: 47.3 us -> 45.5 us  [body(): pl.pallas_call(functools.partial(kernel, n_src, n_unit, nsrc), out_shape=...]
    unnamed x1 -> x0, local copies, waits for them, and re-layouts: 0.6 us -> none
where the time goes in v6:
time: 48.4 us; the launch traced here: 48 us
  Pallas kernels  47.4 us (98%)
  between operations  0.64 us (1%)
    pallas_call x1, Pallas kernels, body(): pl.pallas_call(functools.partial(kernel, n_src, n_unit, nsrc), out_shape=...  45.5 us
    pallas_call x1, Pallas kernels, widen(): pl.pallas_call(functools.partial(widen_kernel, step), out_shape=(jax.Shap...  1.84 us

profile of v6, /device:TPU:1, one launch (start us, length us, event | category | flops | bytes accessed | tf_op | source)
XLA Modules:
  0.0 48.0 jit_solution(5640430323134489802)
XLA Ops:
  0.6 45.5 %shard_map.86 = (bf16[16,448,128]{2,1,0:T(8,128)(2,1)S(1)}, f32[24,55]{1,0:T(8,128)S(1)}) custom-call(bf16[60,1024]{1,0:T(8,128)(2,1)} %bitcast.7, bf16[8,128]{1,0:T(8,128)(2,1)} %bitcast.10, s32[8,128]{1,0:T(8,128)} %bitcast.8, s32[8,128]{1,0:T(8,128)} %bitcast.9, s32[1,24]{1,0:T(1,128)} %cnt_hbm.1, f32[24,55]{1,0:T(8,128)} %coef_hbm.1, ...), custom_call_target="tpu_custom_call" | custom-call | tf_op jit(solution)/shard_map/pallas_call | solution.py:633
  46.2 1.8 %shard_map.87 = (f32[3300,256]{1,0:T(8,128)}, f32[24,55]{1,0:T(8,128)}) custom-call(bf16[16,448,128]{2,1,0:T(8,128)(2,1)S(1)} %get-tuple-element.6.in_ref, f32[24,55]{1,0:T(8,128)S(1)} %get-tuple-element.7.nc_in), custom_call_target="tpu_custom_call" | custom-call | tf_op jit(solution)/shard_map/pallas_call | solution.py:600

commit v7 on v6

--- a/solution.py
+++ b/solution.py
@@ -104,6 +104,7 @@
     rsem4,
     ssem5,
     rsem5,
+    ready,
 ):
     row = lax.axis_index("src")
     me = lax.axis_index("unit")
@@ -137,9 +138,14 @@
     def _(i):
         pl.semaphore_signal(barrier, inc=1, device_id={"unit": unit_at(i)}, device_id_type=MESH)
 
-    @loop(1, n_src)
-    def _(i):
-        pl.semaphore_signal(barrier, inc=1, device_id={"src": row_at(i)}, device_id_type=MESH)
+    px, py = row // side, row % side
+
+    @loop(1, side)
+    def _(i):
+        across = lax.rem(px + i, side) * side + py
+        along = px * side + lax.rem(py + i, side)
+        pl.semaphore_signal(barrier, inc=1, device_id={"src": across}, device_id_type=MESH)
+        pl.semaphore_signal(barrier, inc=1, device_id={"src": along}, device_id_type=MESH)
 
     loads = [
         pltpu.make_async_copy(a, b, lsem.at[n])
@@ -202,7 +208,12 @@
     cown[...] = padded
     crecv[row] = padded
 
-    pl.semaphore_wait(barrier, n_unit + n_src - 2)
+    pl.semaphore_wait(barrier, n_unit - 1 + 2 * (side - 1))
+
+    @loop(1, side)
+    def _(i):
+        along = px * side + lax.rem(py + i, side)
+        pl.semaphore_signal(ready, inc=1, device_id={"src": along}, device_id_type=MESH)
 
     def send1(i):
         return pltpu.make_async_remote_copy(
@@ -244,6 +255,8 @@
         @pl.when(i > 0)
         def _():
             send1(i).start()
+
+    pl.semaphore_wait(ready, side - 1)
 
     @loop(1, n_src)
     def _(i):
@@ -396,7 +409,6 @@
         dk_ref[owner_rows : eflat.shape[0], :] = jnp.zeros((eflat.shape[0] - owner_rows, LANES), F32)
     eflat[...] = dk_ref[0 : eflat.shape[0], :].astype(BF)
 
-    px, py = row // side, row % side
     part_piece = half_rows // 2
 
     def at_offset(half, first, second):
@@ -449,6 +461,11 @@
         def _():
             for n, way in enumerate((two, 1, back)):
                 pass_on(half, row, None, at_offset(half, way, 0), (side, n)).start()
+
+    for half in range(2):
+
+        @pl.when(whole(half, row))
+        def _():
             send_block(half, 0)
 
     gh_ref[...] = jnp.zeros_like(gh_ref)
@@ -684,6 +701,7 @@
             sems((n_unit,)),
             sems((2, side + 1, 5)),
             sems((2, n_src, 2)),
+            pltpu.SemaphoreType.REGULAR,
         ],
         compiler_params=pltpu.CompilerParams(
             collective_id=0, has_side_effects=True, vmem_limit_bytes=44 * 1024 * 1024

time: 48.4 us -> 47.4 us (0.979)
  Pallas kernels: 47.4 us -> 46.7 us
    pallas_call x1, Pallas kernels: 45.5 us -> 44.8 us  [body(): pl.pallas_call(functools.partial(kernel, n_src, n_unit, nsrc), out_shape=...]
where the time goes in v7:
time: 47.4 us; the launch traced here: 47.3 us
  Pallas kernels  46.7 us (99%)
  between operations  0.64 us (1%)
    pallas_call x1, Pallas kernels, body(): pl.pallas_call(functools.partial(kernel, n_src, n_unit, nsrc), out_shape=...  44.8 us
    pallas_call x1, Pallas kernels, widen(): pl.pallas_call(functools.partial(widen_kernel, step), out_shape=(jax.Shap...  1.84 us

profile of v7, /device:TPU:1, one launch (start us, length us, event | category | flops | bytes accessed | tf_op | source)
XLA Modules:
  0.0 47.3 jit_solution(13338235936615046857)
XLA Ops:
  0.6 44.8 %shard_map.86 = (bf16[16,448,128]{2,1,0:T(8,128)(2,1)S(1)}, f32[24,55]{1,0:T(8,128)S(1)}) custom-call(bf16[60,1024]{1,0:T(8,128)(2,1)} %bitcast.7, bf16[8,128]{1,0:T(8,128)(2,1)} %bitcast.10, s32[8,128]{1,0:T(8,128)} %bitcast.8, s32[8,128]{1,0:T(8,128)} %bitcast.9, s32[1,24]{1,0:T(1,128)} %cnt_hbm.1, f32[24,55]{1,0:T(8,128)} %coef_hbm.1, ...), custom_call_target="tpu_custom_call" | custom-call | tf_op jit(solution)/shard_map/pallas_call | solution.py:650
  45.5 1.8 %shard_map.87 = (f32[3300,256]{1,0:T(8,128)}, f32[24,55]{1,0:T(8,128)}) custom-call(bf16[16,448,128]{2,1,0:T(8,128)(2,1)S(1)} %get-tuple-element.6.in_ref, f32[24,55]{1,0:T(8,128)S(1)} %get-tuple-element.7.nc_in), custom_call_target="tpu_custom_call" | custom-call | tf_op jit(solution)/shard_map/pallas_call | solution.py:617

commit v8 on v7

--- a/solution.py
+++ b/solution.py
@@ -539,6 +539,24 @@
     ring(1)
     ring(back)
 
+    @loop(1, n_unit)
+    def _(i):
+        send1(i).wait_send()
+
+    @loop(1, n_src)
+    def _(i):
+        send_coef(i).wait_send()
+        send3(i).wait_send()
+        other = row_at(i)
+        by_group(other % groups, lambda rows: copy2(other, row, rows).wait_send())
+
+    for half in range(2):
+
+        @pl.when(whole(half, row))
+        def _():
+            for n in range(3):
+                pass_on(half, row, None, at_offset(half, 1, 0), (side, n)).wait_send()
+
     for q in range(side):
         for half in range(2):
             for way in (two,) if q in relayed else (1, back, two):
@@ -563,15 +581,7 @@
 
     @loop(1, n_unit)
     def _(i):
-        send1(i).wait_send()
         send4(i).wait_send()
-
-    @loop(1, n_src)
-    def _(i):
-        send_coef(i).wait_send()
-        send3(i).wait_send()
-        other = row_at(i)
-        by_group(other % groups, lambda rows: copy2(other, row, rows).wait_send())
 
     for half in range(2):
         for q in range(side):
@@ -587,11 +597,6 @@
                     @pl.when(whole(half, at_offset(half, q, (back, 1)[n])))
                     def _():
                         pass_on(half, row, n, at_offset(half, 1, 0), (q, 3 + n)).wait_send()
-
-        @pl.when(whole(half, row))
-        def _():
-            for n in range(3):
-                pass_on(half, row, None, at_offset(half, 1, 0), (side, n)).wait_send()
 
 
 def widen_kernel(step, in_ref, nc_in, out_hbm, nc_hbm, wide_ref, sems):

time: 47.4 us -> 47.1 us (level)
  no operation moved by 1% of the time
where the time goes in v8:
time: 47.1 us; the launch traced here: 47 us
  Pallas kernels  46.3 us (98%)
  between operations  0.64 us (1%)
    pallas_call x1, Pallas kernels, body(): pl.pallas_call(functools.partial(kernel, n_src, n_unit, nsrc), out_shape=...  44.5 us
    pallas_call x1, Pallas kernels, widen(): pl.pallas_call(functools.partial(widen_kernel, step), out_shape=(jax.Shap...  1.84 us

profile of v8, /device:TPU:1, one launch (start us, length us, event | category | flops | bytes accessed | tf_op | source)
XLA Modules:
  0.0 47.0 jit_solution(868127925487658749)
XLA Ops:
  0.6 44.5 %shard_map.86 = (bf16[16,448,128]{2,1,0:T(8,128)(2,1)S(1)}, f32[24,55]{1,0:T(8,128)S(1)}) custom-call(bf16[60,1024]{1,0:T(8,128)(2,1)} %bitcast.7, bf16[8,128]{1,0:T(8,128)(2,1)} %bitcast.10, s32[8,128]{1,0:T(8,128)} %bitcast.8, s32[8,128]{1,0:T(8,128)} %bitcast.9, s32[1,24]{1,0:T(1,128)} %cnt_hbm.1, f32[24,55]{1,0:T(8,128)} %coef_hbm.1, ...), custom_call_target="tpu_custom_call" | custom-call | tf_op jit(solution)/shard_map/pallas_call | solution.py:655
  45.1 1.8 %shard_map.87 = (f32[3300,256]{1,0:T(8,128)}, f32[24,55]{1,0:T(8,128)}) custom-call(bf16[16,448,128]{2,1,0:T(8,128)(2,1)S(1)} %get-tuple-element.6.in_ref, f32[24,55]{1,0:T(8,128)S(1)} %get-tuple-element.7.nc_in), custom_call_target="tpu_custom_call" | custom-call | tf_op jit(solution)/shard_map/pallas_call | solution.py:622
